TPU v7x, 256 devices: a whole 4x4x8 slice. The times are simulated.
256 devices in a mesh: col: 8 (over y, x_hi), sec: 32 (over x_lo, z, core).
Axes of the slice: x: 4 (x_hi: 2, x_lo: 2; x = x_hi * 2 + x_lo), y: 4, z: 8, core: 2. Of those that a mesh axis runs over, the one named last changes fastest.
Arguments:
- corner: bfloat16 [8, 64, 4096], P('col', 'sec'), may hold values from -6 to 6
- edge: bfloat16 [8, 256, 64, 4096], P('col', 'sec'), may hold values from -0.75 to 0.75
- closing: bfloat16 [8, 256, 64, 4096], P('col', 'sec'), may hold values from -0.09375 to 0.09375
- projector: float32 [8, 64, 4096], P('col', 'sec'), may hold values from -0.75 to 0.75
- left_slot: int32 [8, 256], P('col', 'sec'), may hold values from 0 to 1
- out_sector: int32 [8, 256], P('col', 'sec'), may hold values from 0 to 63
- owner: int32 [64], replicated, may hold values from 0 to 31, as said below
Outputs:
- new_corner: float32 [8, 64, 4096], P('col', 'sec')
Inputs may be any that keep to these rules, and one draw needn't show every extreme that they name: `owner`: every index of sec owns exactly 2 sectors.
All inputs are finite; a program needn't handle non-finite values. Where the computation divides by a largest or mean magnitude, that divisor is 1e-20 or more.
Results may differ from a plain program's by a relative error of at most 0.0031.
Values sent between devices are 32-bit elements; how exact they have to be, the bound alone decides.
No kernel may reach another device: no remote copies, remote signals or barrier semaphores. Data moves between devices by JAX's collectives and lax.ppermute only.
A program may use at most 64 MiB of HBM per device.

v0:
```python
import jax
import jax.numpy as jnp
from jax import lax
from jax.sharding import PartitionSpec as P

B = 64


def passed_along(value, axis, by):
    count = lax.axis_size(axis)
    return lax.ppermute(value, axis, [(i, (i + by) % count) for i in range(count)])


def pick_corners(corner, left_slot):
    select = (left_slot[:, None] == jnp.arange(corner.shape[0], dtype=jnp.int32)[None, :]).astype(
        jnp.bfloat16
    )
    return jnp.dot(select, corner, preferred_element_type=jnp.float32).astype(jnp.bfloat16)


def block_products(flat_corners, edge, closing):
    count = edge.shape[0]
    left = flat_corners.reshape(count, B, B)
    enlarged = jnp.einsum("kab,kbw->kaw", left, edge, preferred_element_type=jnp.float32).astype(
        jnp.bfloat16
    )
    product = jnp.einsum("kaw,kcw->kac", enlarged, closing, preferred_element_type=jnp.float32)
    return product.reshape(count, B * B)


def local(corner, edge, closing, projector, left_slot, out_sector, owner):
    corner = corner[0]
    edge = edge[0]
    closing = closing[0]
    projector = projector[0]
    left_slot = left_slot[0]
    out_sector = out_sector[0]
    owned_count = corner.shape[0]
    order = jnp.argsort(owner, stable=True)
    picked = pick_corners(corner, left_slot)
    product = block_products(picked, edge, closing)
    placing = (order[:, None] == out_sector[None, :]).astype(jnp.float32)
    partial_value = jnp.dot(placing, product, precision=lax.Precision.HIGHEST)
    joined = lax.psum_scatter(partial_value, "sec", scatter_dimension=0, tiled=True)
    blocks = joined.reshape(owned_count, B, B)
    proj_blocks = projector.reshape(owned_count, B, B)
    inner = jnp.einsum("sba,sbc->sac", proj_blocks, blocks, precision=lax.Precision.HIGHEST)
    projected = jnp.einsum("sac,scd->sad", inner, proj_blocks, precision=lax.Precision.HIGHEST)
    largest = lax.pmax(jnp.max(jnp.abs(projected)), "sec")
    normed = (projected / (largest + 1e-06)).reshape(owned_count, B * B)
    moved = passed_along(normed, "col", 1)
    return moved[None]


def solution(mesh):
    in_specs = (
        P("col", "sec", None),
        P("col", "sec", None, None),
        P("col", "sec", None, None),
        P("col", "sec", None),
        P("col", "sec"),
        P("col", "sec"),
        P(),
    )
    out_specs = P("col", "sec", None)
    return jax.shard_map(local, mesh=mesh, in_specs=in_specs, out_specs=out_specs, check_vma=False)
```

profile of v0, /device:TPU:2, one launch (start us, length us, event | category | flops | bytes accessed | tf_op | source)
XLA Modules:
  0.0 319.9 jit_solution(9328019297185192801)
XLA Ops:
  6.5 0.0 copy-start
  6.5 0.0 all-reduce.3.cloned.1.call-start
  6.5 0.7 copy-done
  7.3 0.9 convolution_convert_fusion.1
  8.1 0.2 reshape.14
  8.3 0.0 copy-start.3
  8.3 0.0 copy-start.2
  8.3 0.0 copy-start.1
  8.3 0.0 copy-start.4
  8.3 5.8 %fusion = f32[8,64,64]{2,1,0:T(8,128)S(1)} fusion(bf16[1,8,64,4096]{3,2,1,0:T(8,128)(2,1)} %param.9, bf16[8,64,64]{2,1,0:T(8,128)(2,1)S(1)} %reshape.14, bf16[1,8,64,4096]{3,2,1,0:T(8,128)(2,1)} %param.8), kind=kOutput, calls=%fused_computation.2 | convolution fusion | flops 538968064 | bytes 8585216 | tf_op jit(solution)/shard_map/kaw,kcw->kac/dot_general | solution.py:27
  14.2 0.1 reshape.15
  14.3 0.0 copy-done.3
  14.3 2.0 sort.17
  16.3 0.0 copy-done.2
  16.3 1.7 fusion.5
  18.0 0.0 all-reduce.3.cloned.1.call-update
  18.0 0.0 copy-done.1
  18.0 0.1 reshape_squeeze.3
  18.1 0.0 copy-done.4
  18.1 0.6 dynamic-slice
  19.4 225.2 %all-reduce.3.cloned.1.call-done = f32[64,4096]{1,0:T(8,128)} async-done(((f32[64,4096]{1,0:T(8,128)}), f32[64,4096]{1,0:T(8,128)}) %all-reduce.3.cloned.1.call-update) | async-done | bytes 1048592
  244.6 0.9 constant_dynamic-slice_fusion
  245.5 0.1 reshape.16
  245.6 0.3 fusion.11
  245.9 0.8 abs_reduce_fusion
  246.7 57.4 %pmax.7 = f32[]{:T(128)} all-reduce(f32[]{:T(128)} %get-tuple-element.7), channel_id=1, replica_groups=mesh['col'=8,'sec'=32] {'sec'}, use_global_device_ids=true, to_apply=%region_3.4 | all-reduce | flops 1 | bytes 8 | tf_op jit(solution)/shard_map/pmax | solution.py:49
  304.7 0.1 reshape.17
  304.8 2.5 collective-permute-start
  307.3 5.2 %collective-permute-done = f32[2,4096]{1,0:T(2,128)S(1)} collective-permute-done((f32[2,4096]{1,0:T(2,128)S(1)}, f32[2,4096]{1,0:T(2,128)S(1)}, u32[]{:S(2)}, u32[]{:S(2)}) %collective-permute-start) | collective-permute-done | bytes 32800 | tf_op jit(solution)/shard_map/ppermute | solution.py:11
  312.4 0.6 copy.10
  (2 shorter events, 0.0 us)
Async XLA Ops:
  6.5 0.7 copy-start
  6.5 238.0 %all-reduce.3.cloned.1.call-start = ((), (), s32[]{:S(2)}) async-start(), calls=%async_computation | async-start | bytes 2097152
  8.3 6.0 %copy-start.3 = (s32[64]{0:T(128)S(1)}, s32[64]{0:T(128)}, u32[]{:S(2)}) copy-start(s32[64]{0:T(128)} %param.13) | copy-start | bytes 772
  8.3 8.0 %copy-start.2 = (s32[1,8]{1,0:T(1,128)S(1)}, s32[1,8]{1,0:T(1,128)}, u32[]{:S(2)}) copy-start(s32[1,8]{1,0:T(1,128)} %param.12) | copy-start | bytes 100
  8.3 9.7 %copy-start.1 = (f32[1,2,4096]{2,1,0:T(2,128)S(1)}, f32[1,2,4096]{2,1,0:T(2,128)}, u32[]{:S(2)}) copy-start(f32[1,2,4096]{2,1,0:T(2,128)} %param.10) | copy-start | bytes 98308
  8.3 9.8 %copy-start.4 = (u32[256]{0:T(256)S(1)}, u32[256]{0:T(256)}, u32[]{:S(2)}) copy-start(u32[256]{0:T(256)} %constant.12) | copy-start | bytes 3076
  304.8 7.6 %collective-permute-start = (f32[2,4096]{1,0:T(2,128)S(1)}, f32[2,4096]{1,0:T(2,128)S(1)}, u32[]{:S(2)}, u32[]{:S(2)}) collective-permute-start(f32[2,4096]{1,0:T(2,128)S(1)} %reshape.17), channel_id=1, source_target_pairs={{0,32},{32,64},{64,96},{96,128},{128,160},{160,192},{192,224},{224... | collective-permute-start | bytes 98312 | tf_op jit(solution)/shard_map/ppermute | solution.py:11
Sparse Core Ops, SparseCore 0:
  18.1 226.3 all-reduce.2
where the time goes:
time: 320 us
  waiting for transfers between devices  230 us (72%)
  blocking collectives  57.4 us (18%)
  between operations  14.8 us (5%)
  matrix products  9.41 us (3%)
  local copies, waits for them, and re-layouts  3.46 us (1%)
    unnamed x2, waiting for transfers between devices  225 us
    pmax x1, blocking collectives, local(): largest = lax.pmax(jnp.max(jnp.abs(projected)), 'sec')  57.4 us
  transfers between devices with their start and end apart: 2, of which 2 were waited for; matrix products, arithmetic and copies ran while one was open for 0% of the time, Pallas kernels for 0%

commit v1 on v0

v1 whole, which is shorter than its diff:
```python
import jax
import jax.numpy as jnp
from jax import lax
from jax.experimental import pallas as pl
from jax.experimental.pallas import tpu as pltpu
from jax.sharding import Mesh, PartitionSpec as P

B = 64
WIDE = 4096
PAIRS = 8
GROUP = 4
TILES = PAIRS // 2
CHUNK = 1024
CHUNKS = WIDE // CHUNK
ROWS = GROUP * B
MSG = TILES * B
SWAP = [(0, 1), (1, 0)]


def low_lanes(shape):
    return lax.broadcasted_iota(jnp.int32, shape, len(shape) - 1) < B


def products_kernel(left_ref, out_ref, owner_ref, corner_ref, edge_ref, closing_ref, msg_ref, edge_buf, closing_buf, lhs_ref, first_ref, edge_sem, closing_sem):
    copies = []
    for g in range(PAIRS // GROUP):
        for w in range(CHUNKS):
            at = (pl.ds(g * ROWS, ROWS), pl.ds(w * CHUNK, CHUNK))
            pair = (
                pltpu.make_async_copy(edge_ref.at[at], edge_buf.at[at], edge_sem.at[g, w]),
                pltpu.make_async_copy(closing_ref.at[at], closing_buf.at[at], closing_sem.at[g, w]),
            )
            pair[0].start()
            pair[1].start()
            copies.append(pair)

    sectors = 2 * 32
    for s in range(sectors - 1, -1, -1):
        first_ref[owner_ref[s]] = s
    slots = []
    for k in range(PAIRS):
        sector = out_ref[k]
        own = owner_ref[sector]
        slots.append((2 * own + jnp.where(first_ref[own] == sector, 0, 1)).astype(jnp.float32))
    low_row = low_lanes((1, 2 * B))
    for t in range(TILES):
        a, b = slots[2 * t], slots[2 * t + 1]
        msg_ref[pl.ds(MSG + 2 * t, 1), :] = jnp.where(low_row, a, b)
        msg_ref[pl.ds(MSG + 2 * t + 1, 1), :] = jnp.where(low_row, b, a)

    low = low_lanes((B, 2 * B))
    lhs_ref[...] = jnp.zeros_like(lhs_ref)
    for k in range(PAIRS):
        i = k % GROUP
        block = corner_ref[left_ref[k]].astype(jnp.float32)
        both = jnp.concatenate([block, block], axis=1)
        mine = jnp.where(low if i % 2 == 0 else ~low, both, 0.0).astype(jnp.bfloat16)
        lhs_ref[pl.ds(k * B, B), pl.ds((i // 2) * 2 * B, 2 * B)] = mine

    for g in range(PAIRS // GROUP):
        total = None
        for w in range(CHUNKS):
            pair = copies[g * CHUNKS + w]
            at = (pl.ds(g * ROWS, ROWS), pl.ds(w * CHUNK, CHUNK))
            pair[0].wait()
            enlarged = jnp.dot(lhs_ref[pl.ds(g * ROWS, ROWS), :], edge_buf[at], preferred_element_type=jnp.float32).astype(jnp.bfloat16)
            pair[1].wait()
            part = lax.dot_general(enlarged, closing_buf[at], (((1,), (1,)), ((), ())), preferred_element_type=jnp.float32)
            total = part if total is None else total + part
        for h in range(GROUP // 2):
            lanes = slice(h * 2 * B, (h + 1) * 2 * B)
            top = total[2 * h * B : (2 * h + 1) * B, lanes]
            bottom = total[(2 * h + 1) * B : (2 * h + 2) * B, lanes]
            msg_ref[pl.ds((g * GROUP // 2 + h) * B, B), :] = jnp.where(low, top, bottom)


def place_kernel(own_ref, other_ref, out_ref, turned_ref):
    dests = out_ref.shape[0]
    core = lax.axis_index("core")
    refs = (own_ref, other_ref)
    for i, ref in enumerate(refs):
        for t in range(TILES):
            turned_ref[i, t] = pltpu.roll(ref[pl.ds(t * B, B), :], B, 1)
    half = jnp.where(low_lanes((1, 2 * B)), 0, 1)
    for d in range(dests):
        slot = (4 * d + 2 * core + half).astype(jnp.float32)
        total = jnp.zeros((B, 2 * B), jnp.float32)
        for i, ref in enumerate(refs):
            for t in range(TILES):
                straight = ref[pl.ds(MSG + 2 * t, 1), :] == slot
                crossed = ref[pl.ds(MSG + 2 * t + 1, 1), :] == slot
                total = total + jnp.where(straight, ref[pl.ds(t * B, B), :], 0.0)
                total = total + jnp.where(crossed, turned_ref[i, t], 0.0)
        out_ref[d] = total


def project_kernel(parts_ref, projector_ref, out_ref, top_ref):
    joined = parts_ref[0]
    for i in range(1, parts_ref.shape[0]):
        joined = joined + parts_ref[i]
    low = low_lanes((B, 2 * B))
    beside = jnp.concatenate([projector_ref[0], projector_ref[1]], axis=1)

    def diagonal(packed):
        return jnp.concatenate([jnp.where(low, packed, 0.0), jnp.where(low, 0.0, packed)], axis=0)

    proj = diagonal(beside)
    inner = jnp.dot(diagonal(joined), proj, precision=lax.Precision.HIGHEST, preferred_element_type=jnp.float32)
    full = lax.dot_general(proj, inner, (((0,), (0,)), ((), ())), precision=lax.Precision.HIGHEST, preferred_element_type=jnp.float32)
    packed = jnp.where(low, full[:B], full[B:])
    out_ref[...] = packed
    size = jnp.abs(packed)
    top = size[:8]
    for i in range(1, 8):
        top = jnp.maximum(top, size[8 * i : 8 * i + 8])
    top_ref[...] = top


VMEM = pl.BlockSpec(memory_space=pltpu.VMEM)
SMEM = pl.BlockSpec(memory_space=pltpu.SMEM)
ANY = pl.BlockSpec(memory_space=pl.ANY)
F32 = jnp.float32


def local(corner, edge, closing, projector, left_slot, out_sector, owner):
    corner = corner.reshape(2, B, B)
    projector = projector.reshape(2, B, B)
    message = pl.pallas_call(
        products_kernel,
        out_shape=jax.ShapeDtypeStruct((MSG + 8, 2 * B), F32),
        in_specs=[SMEM, SMEM, SMEM, VMEM, ANY, ANY],
        out_specs=VMEM,
        scratch_shapes=[
            pltpu.VMEM((PAIRS * B, WIDE), jnp.bfloat16),
            pltpu.VMEM((PAIRS * B, WIDE), jnp.bfloat16),
            pltpu.VMEM((PAIRS * B, ROWS), jnp.bfloat16),
            pltpu.SMEM((32,), jnp.int32),
            pltpu.SemaphoreType.DMA((PAIRS // GROUP, CHUNKS)),
            pltpu.SemaphoreType.DMA((PAIRS // GROUP, CHUNKS)),
        ],
        compiler_params=pltpu.CompilerParams(vmem_limit_bytes=24 << 20),
        name="products",
    )(left_slot[0], out_sector[0], owner, corner, edge.reshape(PAIRS * B, WIDE), closing.reshape(PAIRS * B, WIDE))
    other = lax.ppermute(message, "core", SWAP)
    placed = pl.pallas_call(
        place_kernel,
        out_shape=jax.ShapeDtypeStruct((16, B, 2 * B), F32),
        in_specs=[VMEM, VMEM],
        out_specs=VMEM,
        scratch_shapes=[pltpu.VMEM((2, TILES, B, 2 * B), F32)],
        name="place",
    )(message, other)
    parts = lax.all_to_all(placed, ("xl", "z"), 0, 0)
    packed, top = pl.pallas_call(
        project_kernel,
        out_shape=(jax.ShapeDtypeStruct((B, 2 * B), F32), jax.ShapeDtypeStruct((8, 2 * B), F32)),
        in_specs=[VMEM, VMEM],
        out_specs=(VMEM, VMEM),
        name="project",
    )(parts, projector)
    ahead = [(i, (i + 1) % 8) for i in range(8)]
    blocks = packed.reshape(B, 2, B).transpose(1, 0, 2).reshape(2, B * B)
    moved = lax.ppermute(blocks, "col", ahead)
    top = jnp.maximum(top, lax.ppermute(top, "core", SWAP))
    top = lax.ppermute(top, "col", ahead)
    tops = lax.all_to_all(jnp.broadcast_to(top[None], (16, 8, 2 * B)), ("xl", "z"), 0, 0)
    return (moved / (jnp.max(tops) + 1e-06))[None]


def solution(mesh):
    fine = Mesh(mesh.devices.reshape(8, 2, 8, 2), ("col", "xl", "z", "core"))
    sec = ("xl", "z", "core")
    in_specs = (
        P("col", sec, None),
        P("col", sec, None, None),
        P("col", sec, None, None),
        P("col", sec, None),
        P("col", sec),
        P("col", sec),
        P(),
    )
    return jax.shard_map(local, mesh=fine, in_specs=in_specs, out_specs=P("col", sec, None), check_vma=False)
```

time: 320 us -> 73 us (0.23)
  waiting for transfers between devices: 230 us -> 28.3 us
  blocking collectives: 57.4 us -> 0 us
  starting transfers between devices: 2.45 us -> 17.9 us
  between operations: 14.8 us -> 0.73 us
  Pallas kernels: 0 us -> 12.7 us
  matrix products: 9.41 us -> 0 us
  local copies, waits for them, and re-layouts: 3.46 us -> 10.9 us
    unnamed x2 -> x0, waiting for transfers between devices: 225 us -> none
    pmax x1 -> x0, blocking collectives: 57.4 us -> none  [local(): largest = lax.pmax(jnp.max(jnp.abs(projected)), 'sec')]
    all_to_all x0 -> x2, waiting for transfers between devices: none -> 20.5 us  [the longest x1 14.2 us: local(): parts = lax.all_to_all(placed, ('xl', 'z'), 0, 0)]
    all_to_all x0 -> x2, starting transfers between devices: none -> 15.6 us  [the longest x1 9.94 us: local(): parts = lax.all_to_all(placed, ('xl', 'z'), 0, 0)]
    pallas_call x0 -> x3, Pallas kernels: none -> 12.7 us  [the longest x1 7.85 us: local(): pl.pallas_call(products_kernel, out_shape=jax.ShapeDtypeStruct((MSG + 8,...]
    dot_general x5 -> x0, matrix products: 9.41 us -> none  [the longest x1 5.82 us: block_products(): jnp.einsum('kaw,kcw->kac', enlarged, closing, preferred_element_type=jnp....]
    unnamed x13 -> x18, local copies, waits for them, and re-layouts: 2.86 us -> 7.79 us
    ppermute x1 -> x4, waiting for transfers between devices: 5.15 us -> 7.81 us  [the longest x1 5.1 us: local(): top = lax.ppermute(top, 'col', ahead)]
  transfers between devices with their start and end apart: 2 -> 6, of which waited for: 2 -> 5; matrix products, arithmetic and copies ran while one was open for 0% -> 3% of each run, Pallas kernels for 0% -> 0%
where the time goes in v1:
time: 73 us; the launch traced here: 72.4 us
  waiting for transfers between devices  28.3 us (39%)
  starting transfers between devices  17.9 us (25%)
  Pallas kernels  12.7 us (17%)
  local copies, waits for them, and re-layouts  10.9 us (15%)
  other arithmetic  1.92 us (3%)
  between operations  0.73 us (1%)
    all_to_all x1, waiting for transfers between devices, local(): parts = lax.all_to_all(placed, ('xl', 'z'), 0, 0)  14.2 us
    all_to_all x1, starting transfers between devices, local(): parts = lax.all_to_all(placed, ('xl', 'z'), 0, 0)  9.94 us
    pallas_call x1, Pallas kernels, local(): pl.pallas_call(products_kernel, out_shape=jax.ShapeDtypeStruct((MSG + 8,...  7.85 us
    unnamed x18, local copies, waits for them, and re-layouts  7.79 us
    all_to_all x1, waiting for transfers between devices, local(): lax.all_to_all(jnp.broadcast_to(top[None], (16, 8, 2 * B)), ('xl', 'z'),...  6.3 us
    all_to_all x1, starting transfers between devices, local(): lax.all_to_all(jnp.broadcast_to(top[None], (16, 8, 2 * B)), ('xl', 'z'),...  5.66 us
    ppermute x1, waiting for transfers between devices, local(): top = lax.ppermute(top, 'col', ahead)  5.1 us
    pallas_call x1, Pallas kernels, local(): pl.pallas_call(place_kernel, out_shape=jax.ShapeDtypeStruct((16, B, 2 * B...  2.66 us
  transfers between devices with their start and end apart: 6, of which 5 were waited for; matrix products, arithmetic and copies ran while one was open for 3% of the time, Pallas kernels for 0%

profile of v1, /device:TPU:2, one launch (start us, length us, event | category | flops | bytes accessed | tf_op | source)
XLA Modules:
  0.0 72.4 jit_solution(15724532203072467633)
XLA Ops:
  0.0 0.8 %reshape.19.corner_ref = bf16[2,64,64]{2,1,0:T(8,128)(2,1)S(1)} reshape(bf16[1,2,4096]{2,1,0:T(2,128)(2,1)} %param.7) | data formatting | bytes 32768 | tf_op jit(solution)/shard_map/reshape | solution.py:126
  0.8 0.0 copy-start
  0.8 2.2 %copy-done = bf16[1,8,64,4096]{3,2,1,0:T(8,128)(2,1)S(1)} copy-done((bf16[1,8,64,4096]{3,2,1,0:T(8,128)(2,1)S(1)}, bf16[1,8,64,4096]{3,2,1,0:T(8,128)(2,1)}, u32[]{:S(2)}) %copy-start) | copy-done | bytes 4194328
  3.0 2.2 %copy-done.1 = bf16[1,8,64,4096]{3,2,1,0:T(8,128)(2,1)S(1)} copy-done((bf16[1,8,64,4096]{3,2,1,0:T(8,128)(2,1)S(1)}, bf16[1,8,64,4096]{3,2,1,0:T(8,128)(2,1)}, u32[]{:S(2)}) %copy-start.1) | copy-done | bytes 4194328
  5.2 0.7 copy-done.3
  5.8 0.7 copy-done.4
  6.5 0.7 copy-done.5
  7.2 7.9 %products.1.own_ref = f32[264,128]{1,0:T(8,128)S(1)} custom-call(s32[8]{0:T(128)S(1)} %bitcast.9, s32[8]{0:T(128)S(1)} %bitcast.10, s32[64]{0:T(128)S(1)} %copy-done.5, bf16[2,64,64]{2,1,0:T(8,128)(2,1)S(1)} %reshape.19.corner_ref, bf16[512,4096]{1,0:T(8,128)(2,1)S(1)} %bitcast.7, bf16[512,4096]{1,0:T(8,128)(2,1)S(1)} %bitcast.8), custom_call_target="tpu_custom_call" | custom-call | tf_op jit(solution)/shard_map/products/pallas_call | solution.py:128
  15.0 0.0 copy-start.2
  15.0 0.1 collective-permute-start
  15.1 1.3 %collective-permute-done.other_ref = f32[264,128]{1,0:T(8,128)S(1)} collective-permute-done((f32[264,128]{1,0:T(8,128)S(1)}, f32[264,128]{1,0:T(8,128)S(1)}, u32[]{:S(2)}, u32[]{:S(2)}) %collective-permute-start) | collective-permute-done | bytes 135200 | tf_op jit(solution)/shard_map/ppermute | solution.py:144
  16.5 0.7 copy-done.7
  17.1 2.7 %place.1 = f32[16,64,128]{2,1,0:T(8,128)} custom-call(f32[264,128]{1,0:T(8,128)} %copy-done.2, f32[264,128]{1,0:T(8,128)} %copy-done.7), custom_call_target="tpu_custom_call" | custom-call | tf_op jit(solution)/shard_map/place/pallas_call | solution.py:145
  19.8 9.9 %all-to-all-start = ((f32[16,64,128]{2,1,0:T(8,128)}), f32[16,64,128]{2,1,0:T(8,128)S(1)}, u32[]{:S(2)}, u32[]{:S(2)}) async-start(f32[16,64,128]{2,1,0:T(8,128)} %place.1), calls=%async_computation | async-start | bytes 1048576 | tf_op jit(solution)/shard_map/all_to_all | solution.py:153
  29.7 0.7 reshape.22.projector_ref
  30.5 14.2 %all-to-all-done.parts_ref = f32[16,64,128]{2,1,0:T(8,128)S(1)} async-done(((f32[16,64,128]{2,1,0:T(8,128)}), f32[16,64,128]{2,1,0:T(8,128)S(1)}, u32[]{:S(2)}, u32[]{:S(2)}) %all-to-all-start) | async-done | bytes 524320 | tf_op jit(solution)/shard_map/all_to_all | solution.py:153
  44.6 0.8 %copy-done.6 = f32[16,64,128]{2,1,0:T(8,128)} copy-done((f32[16,64,128]{2,1,0:T(8,128)}, f32[16,64,128]{2,1,0:T(8,128)S(1)}, u32[]{:S(2)}) %copy-start.6) | copy-done | bytes 524312
  45.4 2.2 %project.1 = (f32[64,128]{1,0:T(8,128)}, f32[8,128]{1,0:T(8,128)}) custom-call(f32[16,64,128]{2,1,0:T(8,128)} %copy-done.6, f32[2,64,64]{2,1,0:T(8,128)} %reshape.22.projector_ref), custom_call_target="tpu_custom_call" | custom-call | tf_op jit(solution)/shard_map/project/pallas_call | solution.py:154
  47.6 0.0 collective-permute-start.2
  47.6 1.4 %collective-permute-done.2 = f32[8,128]{1,0:T(8,128)S(1)} collective-permute-done((f32[8,128]{1,0:T(8,128)}, f32[8,128]{1,0:T(8,128)S(1)}, u32[]{:S(2)}, u32[]{:S(2)}) %collective-permute-start.2) | collective-permute-done | bytes 4128 | tf_op jit(solution)/shard_map/ppermute | solution.py:164
  49.0 0.7 max.3
  49.7 2.1 %collective-permute-start.3 = (f32[8,128]{1,0:T(8,128)S(1)}, f32[8,128]{1,0:T(8,128)S(1)}, u32[]{:S(2)}, u32[]{:S(2)}) collective-permute-start(f32[8,128]{1,0:T(8,128)S(1)} %max.3), channel_id=1, source_target_pairs={{0,32},{32,64},{64,96},{96,128},{128,160},{160,192},{192,224},{224... | collective-permute-start | bytes 12296 | tf_op jit(solution)/shard_map/ppermute | solution.py:165
  51.8 5.1 %collective-permute-done.3 = f32[8,128]{1,0:T(8,128)S(1)} collective-permute-done((f32[8,128]{1,0:T(8,128)S(1)}, f32[8,128]{1,0:T(8,128)S(1)}, u32[]{:S(2)}, u32[]{:S(2)}) %collective-permute-start.3) | collective-permute-done | bytes 4128 | tf_op jit(solution)/shard_map/ppermute | solution.py:165
  56.9 0.6 broadcast_in_dim.4
  57.5 5.7 %all-to-all-start.1 = ((f32[16,8,128]{2,1,0:T(8,128)}), f32[16,8,128]{2,1,0:T(8,128)S(1)}, u32[]{:S(2)}, u32[]{:S(2)}) async-start(f32[16,8,128]{2,1,0:T(8,128)} %broadcast_in_dim.4), calls=%async_computation.1 | async-start | bytes 131072 | tf_op jit(solution)/shard_map/all_to_all | solution.py:166
  63.2 0.9 %reshape.23 = f32[64,2,64]{2,1,0:T(2,128)S(1)} reshape(f32[64,128]{1,0:T(8,128)} %get-tuple-element.7) | data formatting | bytes 65536 | tf_op jit(solution)/shard_map/reshape | solution.py:162
  64.0 0.1 reshape.24
  64.1 0.1 collective-permute-start.1
  64.2 6.3 %all-to-all-done.1 = f32[16,8,128]{2,1,0:T(8,128)S(1)} async-done(((f32[16,8,128]{2,1,0:T(8,128)}), f32[16,8,128]{2,1,0:T(8,128)S(1)}, u32[]{:S(2)}, u32[]{:S(2)}) %all-to-all-start.1) | async-done | bytes 65568 | tf_op jit(solution)/shard_map/all_to_all | solution.py:166
  70.5 0.6 reduce_max.9
  71.8 0.0 collective-permute-done.1
  71.8 0.6 divide_bitcast_fusion
  (10 shorter events, 0.0 us)
Async XLA Ops:
  0.8 2.2 %copy-start = (bf16[1,8,64,4096]{3,2,1,0:T(8,128)(2,1)S(1)}, bf16[1,8,64,4096]{3,2,1,0:T(8,128)(2,1)}, u32[]{:S(2)}) copy-start(bf16[1,8,64,4096]{3,2,1,0:T(8,128)(2,1)} %param.8) | copy-start | bytes 12582916
  3.0 2.2 %copy-start.1 = (bf16[1,8,64,4096]{3,2,1,0:T(8,128)(2,1)S(1)}, bf16[1,8,64,4096]{3,2,1,0:T(8,128)(2,1)}, u32[]{:S(2)}) copy-start(bf16[1,8,64,4096]{3,2,1,0:T(8,128)(2,1)} %param.9) | copy-start | bytes 12582916
  5.2 0.7 copy-start.3
  5.8 0.7 copy-start.4
  6.5 0.7 copy-start.5
  7.2 22.6 %copy-start.8 = (f32[1,2,4096]{2,1,0:T(2,128)S(1)}, f32[1,2,4096]{2,1,0:T(2,128)}, u32[]{:S(2)}) copy-start(f32[1,2,4096]{2,1,0:T(2,128)} %param.10) | copy-start | bytes 98308
  15.0 1.5 %copy-start.2 = (f32[264,128]{1,0:T(8,128)}, f32[264,128]{1,0:T(8,128)S(1)}, u32[]{:S(2)}) copy-start(f32[264,128]{1,0:T(8,128)S(1)} %products.1.own_ref) | copy-start | bytes 405508
  15.0 1.4 %collective-permute-start = (f32[264,128]{1,0:T(8,128)S(1)}, f32[264,128]{1,0:T(8,128)S(1)}, u32[]{:S(2)}, u32[]{:S(2)}) collective-permute-start(f32[264,128]{1,0:T(8,128)S(1)} %products.1.own_ref), channel_id=1, source_target_pairs={{0,1},{1,0},{2,3},{3,2},{4,5},{5,4},{6,7},{7,6},{8,9},{9,8},{10,11... | collective-permute-start | bytes 405512 | tf_op jit(solution)/shard_map/ppermute | solution.py:144
  16.5 0.7 copy-start.7
  19.8 24.9 %all-to-all-start = ((f32[16,64,128]{2,1,0:T(8,128)}), f32[16,64,128]{2,1,0:T(8,128)S(1)}, u32[]{:S(2)}, u32[]{:S(2)}) async-start(f32[16,64,128]{2,1,0:T(8,128)} %place.1), calls=%async_computation | async-start | bytes 1048576 | tf_op jit(solution)/shard_map/all_to_all | solution.py:153
  44.6 0.8 %copy-start.6 = (f32[16,64,128]{2,1,0:T(8,128)}, f32[16,64,128]{2,1,0:T(8,128)S(1)}, u32[]{:S(2)}) copy-start(f32[16,64,128]{2,1,0:T(8,128)S(1)} %all-to-all-done.parts_ref) | copy-start | bytes 1572868
  47.6 1.4 %collective-permute-start.2 = (f32[8,128]{1,0:T(8,128)}, f32[8,128]{1,0:T(8,128)S(1)}, u32[]{:S(2)}, u32[]{:S(2)}) collective-permute-start(f32[8,128]{1,0:T(8,128)} %get-tuple-element.8), channel_id=1, source_target_pairs={{0,1},{1,0},{2,3},{3,2},{4,5},{5,4},{6,7},{7,6},{8,9},{9,8},{10,11... | collective-permute-start | bytes 12296 | tf_op jit(solution)/shard_map/ppermute | solution.py:164
  49.7 7.2 %collective-permute-start.3 = (f32[8,128]{1,0:T(8,128)S(1)}, f32[8,128]{1,0:T(8,128)S(1)}, u32[]{:S(2)}, u32[]{:S(2)}) collective-permute-start(f32[8,128]{1,0:T(8,128)S(1)} %max.3), channel_id=1, source_target_pairs={{0,32},{32,64},{64,96},{96,128},{128,160},{160,192},{192,224},{224... | collective-permute-start | bytes 12296 | tf_op jit(solution)/shard_map/ppermute | solution.py:165
  57.5 13.0 %all-to-all-start.1 = ((f32[16,8,128]{2,1,0:T(8,128)}), f32[16,8,128]{2,1,0:T(8,128)S(1)}, u32[]{:S(2)}, u32[]{:S(2)}) async-start(f32[16,8,128]{2,1,0:T(8,128)} %broadcast_in_dim.4), calls=%async_computation.1 | async-start | bytes 131072 | tf_op jit(solution)/shard_map/all_to_all | solution.py:166
  64.1 7.7 %collective-permute-start.1 = (f32[2,4096]{1,0:T(2,128)S(1)}, f32[2,4096]{1,0:T(2,128)S(1)}, u32[]{:S(2)}, u32[]{:S(2)}) collective-permute-start(f32[2,4096]{1,0:T(2,128)S(1)} %reshape.24), channel_id=1, source_target_pairs={{0,32},{32,64},{64,96},{96,128},{128,160},{160,192},{192,224},{224... | collective-permute-start | bytes 98312 | tf_op jit(solution)/shard_map/ppermute | solution.py:163

commit v2 on v1

v2 whole, which is shorter than its diff:
```python
import jax
import jax.numpy as jnp
from jax import lax
from jax.experimental import pallas as pl
from jax.experimental.pallas import tpu as pltpu
from jax.sharding import Mesh, PartitionSpec as P

B = 64
WIDE = 4096
PAIRS = 8
TILES = PAIRS // 2
MSG = TILES * B
SECTORS = 64
ZS = 8
AHEAD = 3
SWAP = [(0, 1), (1, 0)]
F32 = jnp.float32
BF16 = jnp.bfloat16


def low_lanes(shape):
    return lax.broadcasted_iota(jnp.int32, shape, len(shape) - 1) < B


def products_kernel(left_hbm, out_hbm, owner_hbm, corner_hbm, edge_hbm, closing_hbm, msg_ref, left_ref, out_ref, owner_ref, first_ref, corner_ref, rows_ref, both_ref, edge_ref, closing_ref, small_sem, edge_sem, closing_sem):
    small = [
        pltpu.make_async_copy(src, dst, small_sem.at[i])
        for i, (src, dst) in enumerate(((corner_hbm, corner_ref), (left_hbm, left_ref), (owner_hbm, owner_ref), (out_hbm, out_ref)))
    ]
    for copy in small:
        copy.start()
    big = []
    for t in range(TILES):
        rows = pl.ds(t * 2 * B, 2 * B)
        big.append((
            pltpu.make_async_copy(edge_hbm.at[rows], edge_ref.at[rows], edge_sem.at[t]),
            pltpu.make_async_copy(closing_hbm.at[rows], closing_ref.at[rows], closing_sem.at[t]),
        ))
    for t in range(AHEAD):
        big[t][0].start()
        big[t][1].start()

    low = low_lanes((B, 2 * B))
    small[0].wait()
    for r in range(2):
        for t in range(B // 2):
            rows_ref[r, pl.ds(t, 1), :] = corner_ref[pl.ds(r, 1), pl.ds(t * 2 * B, 2 * B)].astype(F32)
    low_half = low_lanes((B // 2, 2 * B))
    for r in range(2):
        packed = rows_ref[r]
        turned = pltpu.roll(packed, B, 1)
        both_ref[r, pl.ds(0, B // 2, stride=2), :] = jnp.where(low_half, packed, turned)
        both_ref[r, pl.ds(1, B // 2, stride=2), :] = jnp.where(low_half, turned, packed)
    small[1].wait()
    lefts = []
    for t in range(TILES):
        top = jnp.where(low, both_ref[left_ref[0, 2 * t]], 0.0)
        bottom = jnp.where(low, 0.0, both_ref[left_ref[0, 2 * t + 1]])
        lefts.append(jnp.concatenate([top, bottom], axis=0).astype(BF16))

    small[2].wait()
    for s in range(SECTORS - 1, -1, -1):
        first_ref[owner_ref[s]] = s
    small[3].wait()
    for k in range(PAIRS):
        sector = out_ref[0, k]
        own = owner_ref[sector]
        slot = (2 * own + jnp.where(first_ref[own] == sector, 0, 1)).astype(F32)
        msg_ref[pl.ds(MSG + k, 1), :] = jnp.full((1, 2 * B), slot, F32)

    for t in range(TILES):
        rows = pl.ds(t * 2 * B, 2 * B)
        big[t][0].wait()
        big[t][1].wait()
        if t + AHEAD < TILES:
            big[t + AHEAD][0].start()
            big[t + AHEAD][1].start()
        enlarged = jnp.dot(lefts[t], edge_ref[rows], preferred_element_type=F32).astype(BF16)
        total = lax.dot_general(enlarged, closing_ref[rows], (((1,), (1,)), ((), ())), preferred_element_type=F32)
        msg_ref[pl.ds(t * B, B), :] = jnp.where(low, total[:B], total[B:])


def place_kernel(m0_ref, m1_ref, m2_ref, m3_ref, out_ref, slots_ref, sem):
    refs = (m0_ref, m1_ref, m2_ref, m3_ref)
    copies = [pltpu.make_async_copy(ref.at[pl.ds(MSG, PAIRS)], slots_ref.at[i], sem.at[i]) for i, ref in enumerate(refs)]
    for copy in copies:
        copy.start()
    core, xl = lax.axis_index("core"), lax.axis_index("xl")
    out_ref[...] = jnp.zeros_like(out_ref)
    low = low_lanes((B, 2 * B))
    half = jnp.where(low, 0, 1)
    for copy in copies:
        copy.wait()
    for i, ref in enumerate(refs):
        for k in range(PAIRS):
            slot = slots_ref[i, k, 0].astype(jnp.int32)
            sec = slot >> 1

            @pl.when(((sec & 1) == core) & ((sec >> 4) == xl))
            def _(ref=ref, k=k, slot=slot, sec=sec):
                tile = ref[pl.ds(k // 2 * B, B), :]
                alone = jnp.where(low, tile, 0.0) if k % 2 == 0 else jnp.where(low, 0.0, tile)
                spread = alone + pltpu.roll(alone, B, 1)
                z = (sec >> 1) & (ZS - 1)
                out_ref[z] = out_ref[z] + jnp.where(half == (slot & 1), spread, 0.0)


def project_kernel(parts_ref, projector_ref, out_ref, top_ref):
    joined = parts_ref[0]
    for i in range(1, parts_ref.shape[0]):
        joined = joined + parts_ref[i]
    low = low_lanes((B, 2 * B))
    beside = jnp.concatenate([projector_ref[0], projector_ref[1]], axis=1)

    def diagonal(packed):
        return jnp.concatenate([jnp.where(low, packed, 0.0), jnp.where(low, 0.0, packed)], axis=0)

    proj = diagonal(beside)
    inner = jnp.dot(diagonal(joined), proj, precision=lax.Precision.HIGHEST, preferred_element_type=F32)
    full = lax.dot_general(proj, inner, (((0,), (0,)), ((), ())), precision=lax.Precision.HIGHEST, preferred_element_type=F32)
    packed = jnp.where(low, full[:B], full[B:])
    out_ref[...] = packed
    size = jnp.abs(packed)
    top = size[:8]
    for i in range(1, 8):
        top = jnp.maximum(top, size[8 * i : 8 * i + 8])
    top_ref[...] = top


VMEM = pl.BlockSpec(memory_space=pltpu.VMEM)
ANY = pl.BlockSpec(memory_space=pl.ANY)
SMALL = pltpu.CompilerParams(vmem_limit_bytes=8 << 20)


def local(corner, edge, closing, projector, left_slot, out_sector, owner):
    message = pl.pallas_call(
        products_kernel,
        out_shape=jax.ShapeDtypeStruct((MSG + PAIRS, 2 * B), F32),
        in_specs=[ANY] * 6,
        out_specs=VMEM,
        scratch_shapes=[
            pltpu.SMEM((1, PAIRS), jnp.int32),
            pltpu.SMEM((1, PAIRS), jnp.int32),
            pltpu.SMEM((SECTORS,), jnp.int32),
            pltpu.SMEM((SECTORS // 2,), jnp.int32),
            pltpu.VMEM((2, B * B), BF16),
            pltpu.VMEM((2, B // 2, 2 * B), F32),
            pltpu.VMEM((2, B, 2 * B), F32),
            pltpu.VMEM((PAIRS * B, WIDE), BF16),
            pltpu.VMEM((PAIRS * B, WIDE), BF16),
            pltpu.SemaphoreType.DMA((4,)),
            pltpu.SemaphoreType.DMA((TILES,)),
            pltpu.SemaphoreType.DMA((TILES,)),
        ],
        compiler_params=pltpu.CompilerParams(vmem_limit_bytes=61 << 20),
        name="products",
    )(left_slot, out_sector, owner, corner[0], edge.reshape(PAIRS * B, WIDE), closing.reshape(PAIRS * B, WIDE))
    over = lax.ppermute(message, "xl", SWAP)
    beside = lax.ppermute(message, "core", SWAP)
    across = lax.ppermute(over, "core", SWAP)
    placed = pl.pallas_call(
        place_kernel,
        out_shape=jax.ShapeDtypeStruct((ZS, B, 2 * B), F32),
        in_specs=[VMEM] * 4,
        out_specs=VMEM,
        scratch_shapes=[pltpu.SMEM((4, PAIRS, 2 * B), F32), pltpu.SemaphoreType.DMA((4,))],
        compiler_params=SMALL,
        name="place",
    )(message, beside, over, across)
    parts = lax.all_to_all(placed, "z", 0, 0)
    packed, top = pl.pallas_call(
        project_kernel,
        out_shape=(jax.ShapeDtypeStruct((B, 2 * B), F32), jax.ShapeDtypeStruct((8, 2 * B), F32)),
        in_specs=[VMEM, VMEM],
        out_specs=(VMEM, VMEM),
        compiler_params=SMALL,
        name="project",
    )(parts, projector.reshape(2, B, B))
    ahead = [(i, (i + 1) % 8) for i in range(8)]
    blocks = packed.reshape(B, 2, B).transpose(1, 0, 2).reshape(2, B * B)
    moved = lax.ppermute(blocks, "col", ahead)
    top = jnp.maximum(top, lax.ppermute(top, "core", SWAP))
    top = lax.ppermute(top, "col", ahead)
    tops = lax.all_to_all(jnp.broadcast_to(top[None], (2 * ZS, 8, 2 * B)), ("xl", "z"), 0, 0)
    return (moved / (jnp.max(tops) + 1e-06))[None]


def solution(mesh):
    fine = Mesh(mesh.devices.reshape(8, 2, ZS, 2), ("col", "xl", "z", "core"))
    sec = ("xl", "z", "core")
    in_specs = (
        P("col", sec, None),
        P("col", sec, None, None),
        P("col", sec, None, None),
        P("col", sec, None),
        P("col", sec),
        P("col", sec),
        P(),
    )
    return jax.shard_map(local, mesh=fine, in_specs=in_specs, out_specs=P("col", sec, None), check_vma=False)
```

time: 73 us -> 59.4 us (0.81)
  local copies, waits for them, and re-layouts: 10.9 us -> 1.84 us
  Pallas kernels: 12.7 us -> 8.13 us
  waiting for transfers between devices: 28.3 us -> 30.4 us
  starting transfers between devices: 17.9 us -> 16.8 us
    unnamed x18 -> x4, local copies, waits for them, and re-layouts: 7.79 us -> 0.91 us
    all_to_all x2, starting transfers between devices: 15.6 us -> 12 us  [the longest x1 8.62 us: local(): parts = lax.all_to_all(placed, 'z', 0, 0)]
    ppermute x1 -> x3, waiting for transfers between devices: 1.34 us -> 4.61 us  [the longest x1 3.26 us: local(): over = lax.ppermute(message, 'xl', SWAP)]
    pallas_call x2, Pallas kernels: 10.5 us -> 7.62 us  [the longest x1 5.51 us: local(): pl.pallas_call(products_kernel, out_shape=jax.ShapeDtypeStruct((MSG + PAI...]
    ppermute x1 -> x3, starting transfers between devices: 0.09 us -> 2.36 us  [the longest x1 2.36 us: local(): over = lax.ppermute(message, 'xl', SWAP)]
    pallas_call x1, Pallas kernels: 2.18 us -> 0.52 us  [local(): pl.pallas_call(project_kernel, out_shape=(jax.ShapeDtypeStruct((B, 2 * B)...]
    reshape x2 -> x1, local copies, waits for them, and re-layouts: 1.53 us -> 0.11 us  [local(): projector.reshape(2, B, B)]
    all_to_all x2, waiting for transfers between devices: 20.5 us -> 19.7 us  [the longest x1 12.7 us: local(): parts = lax.all_to_all(placed, 'z', 0, 0)]
  transfers between devices with their start and end apart: 6 -> 8, of which waited for: 5 -> 6; matrix products, arithmetic and copies ran while one was open for 3% -> 2% of each run, Pallas kernels for 0% -> 0%
where the time goes in v2:
time: 59.4 us; the launch traced here: 59.2 us
  waiting for transfers between devices  30.4 us (51%)
  starting transfers between devices  16.8 us (28%)
  Pallas kernels  8.13 us (14%)
  local copies, waits for them, and re-layouts  1.84 us (3%)
  other arithmetic  1.25 us (2%)
  between operations  0.72 us (1%)
    all_to_all x1, waiting for transfers between devices, local(): parts = lax.all_to_all(placed, 'z', 0, 0)  12.7 us
    all_to_all x1, starting transfers between devices, local(): parts = lax.all_to_all(placed, 'z', 0, 0)  8.62 us
    all_to_all x1, waiting for transfers between devices, local(): lax.all_to_all(jnp.broadcast_to(top[None], (2 * ZS, 8, 2 * B)), ('xl', 'z...  6.95 us
    pallas_call x1, Pallas kernels, local(): pl.pallas_call(products_kernel, out_shape=jax.ShapeDtypeStruct((MSG + PAI...  5.51 us
    ppermute x1, waiting for transfers between devices, local(): top = lax.ppermute(top, 'col', ahead)  5.05 us
    all_to_all x1, starting transfers between devices, local(): lax.all_to_all(jnp.broadcast_to(top[None], (2 * ZS, 8, 2 * B)), ('xl', 'z...  3.38 us
    ppermute x1, waiting for transfers between devices, local(): over = lax.ppermute(message, 'xl', SWAP)  3.26 us
    ppermute x1, starting transfers between devices, local(): over = lax.ppermute(message, 'xl', SWAP)  2.36 us
  transfers between devices with their start and end apart: 8, of which 6 were waited for; matrix products, arithmetic and copies ran while one was open for 2% of the time, Pallas kernels for 0%

profile of v2, /device:TPU:2, one launch (start us, length us, event | category | flops | bytes accessed | tf_op | source)
XLA Modules:
  0.0 59.2 jit_solution(7471268424151671526)
XLA Ops:
  0.0 0.0 copy-start.1
  0.0 5.5 %products.1.m0_ref = f32[264,128]{1,0:T(8,128)} custom-call(s32[1,8]{1,0:T(1,128)} %left_hbm.1, s32[1,8]{1,0:T(1,128)} %out_hbm.1, s32[64]{0:T(128)} %owner_hbm.1, bf16[2,4096]{1,0:T(2,128)(2,1)} %bitcast.9, bf16[512,4096]{1,0:T(8,128)(2,1)} %bitcast.6, bf16[512,4096]{1,0:T(8,128)(2,1)} %bitcast.7), custom_call_target="tpu_custom_call" | custom-call | tf_op jit(solution)/shard_map/products/pallas_call | solution.py:136
  5.5 2.4 %collective-permute-start.1 = (f32[264,128]{1,0:T(8,128)}, f32[264,128]{1,0:T(8,128)S(1)}, u32[]{:S(2)}, u32[]{:S(2)}) collective-permute-start(f32[264,128]{1,0:T(8,128)} %products.1.m0_ref), channel_id=1, source_target_pairs={{0,16},{16,0},{1,17},{17,1},{2,18},{18,2},{3,19},{19,3},{4,20},{20... | collective-permute-start | bytes 405512 | tf_op jit(solution)/shard_map/ppermute | solution.py:158
  7.9 0.0 collective-permute-start
  7.9 3.3 %collective-permute-done.1.m2_ref = f32[264,128]{1,0:T(8,128)S(1)} collective-permute-done((f32[264,128]{1,0:T(8,128)}, f32[264,128]{1,0:T(8,128)S(1)}, u32[]{:S(2)}, u32[]{:S(2)}) %collective-permute-start.1) | collective-permute-done | bytes 135200 | tf_op jit(solution)/shard_map/ppermute | solution.py:158
  11.1 0.0 collective-permute-start.2
  11.1 0.0 collective-permute-done.m1_ref
  11.2 1.3 %collective-permute-done.2.m3_ref = f32[264,128]{1,0:T(8,128)S(1)} collective-permute-done((f32[264,128]{1,0:T(8,128)S(1)}, f32[264,128]{1,0:T(8,128)S(1)}, u32[]{:S(2)}, u32[]{:S(2)}) %collective-permute-start.2) | collective-permute-done | bytes 135200 | tf_op jit(solution)/shard_map/ppermute | solution.py:160
  12.5 0.0 copy-start
  12.5 0.9 %copy-done = f32[264,128]{1,0:T(8,128)S(1)} copy-done((f32[264,128]{1,0:T(8,128)S(1)}, f32[264,128]{1,0:T(8,128)}, u32[]{:S(2)}) %copy-start) | copy-done | bytes 135192
  13.4 2.1 %place.1 = f32[8,64,128]{2,1,0:T(8,128)} custom-call(f32[264,128]{1,0:T(8,128)S(1)} %copy-done, f32[264,128]{1,0:T(8,128)S(1)} %collective-permute-done.m1_ref, f32[264,128]{1,0:T(8,128)S(1)} %collective-permute-done.1.m2_ref, f32[264,128]{1,0:T(8,128)S(1)} %collective-permute-done.2.m3_ref), custom_call_target="tpu_custom_call" | custom-call | tf_op jit(solution)/shard_map/place/pallas_call | solution.py:161
  15.5 8.6 %all-to-all-start = ((f32[8,64,128]{2,1,0:T(8,128)}), f32[8,64,128]{2,1,0:T(8,128)S(1)}, u32[]{:S(2)}, u32[]{:S(2)}) async-start(f32[8,64,128]{2,1,0:T(8,128)} %place.1), calls=%async_computation | async-start | bytes 524288 | tf_op jit(solution)/shard_map/all_to_all | solution.py:170
  24.1 0.0 copy-done.1
  24.1 0.1 reshape.18.projector_ref
  24.3 12.7 %all-to-all-done.parts_ref = f32[8,64,128]{2,1,0:T(8,128)S(1)} async-done(((f32[8,64,128]{2,1,0:T(8,128)}), f32[8,64,128]{2,1,0:T(8,128)S(1)}, u32[]{:S(2)}, u32[]{:S(2)}) %all-to-all-start) | async-done | bytes 262176 | tf_op jit(solution)/shard_map/all_to_all | solution.py:170
  37.0 0.5 project.1
  37.5 0.2 collective-permute-start.4
  37.7 1.1 %collective-permute-done.4 = f32[8,128]{1,0:T(8,128)S(1)} collective-permute-done((f32[8,128]{1,0:T(8,128)S(1)}, f32[8,128]{1,0:T(8,128)S(1)}, u32[]{:S(2)}, u32[]{:S(2)}) %collective-permute-start.4) | collective-permute-done | bytes 4128 | tf_op jit(solution)/shard_map/ppermute | solution.py:182
  38.8 2.2 %collective-permute-start.5 = (f32[8,128]{1,0:T(8,128)S(1)}, f32[8,128]{1,0:T(8,128)S(1)}, u32[]{:S(2)}, u32[]{:S(2)}) collective-permute-start(f32[8,128]{1,0:T(8,128)S(1)} %max.3), channel_id=1, source_target_pairs={{0,32},{32,64},{64,96},{96,128},{128,160},{160,192},{192,224},{224... | collective-permute-start | bytes 12296 | tf_op jit(solution)/shard_map/ppermute | solution.py:183
  40.9 5.1 %collective-permute-done.5 = f32[8,128]{1,0:T(8,128)S(1)} collective-permute-done((f32[8,128]{1,0:T(8,128)S(1)}, f32[8,128]{1,0:T(8,128)S(1)}, u32[]{:S(2)}, u32[]{:S(2)}) %collective-permute-start.5) | collective-permute-done | bytes 4128 | tf_op jit(solution)/shard_map/ppermute | solution.py:183
  46.0 0.6 %broadcast_in_dim.4 = f32[16,8,128]{2,1,0:T(8,128)} broadcast(f32[8,128]{1,0:T(8,128)S(1)} %collective-permute-done.5), dimensions={1,2} | broadcast | bytes 69632 | tf_op jit(solution)/shard_map/broadcast_in_dim | solution.py:184
  46.6 3.4 %all-to-all-start.1 = ((f32[16,8,128]{2,1,0:T(8,128)}), f32[16,8,128]{2,1,0:T(8,128)S(1)}, u32[]{:S(2)}, u32[]{:S(2)}) async-start(f32[16,8,128]{2,1,0:T(8,128)} %broadcast_in_dim.4), calls=%async_computation.1 | async-start | bytes 131072 | tf_op jit(solution)/shard_map/all_to_all | solution.py:184
  50.0 0.1 reshape.19
  50.1 0.1 reshape.20
  50.2 0.1 collective-permute-start.3
  50.4 6.9 %all-to-all-done.1 = f32[16,8,128]{2,1,0:T(8,128)S(1)} async-done(((f32[16,8,128]{2,1,0:T(8,128)}), f32[16,8,128]{2,1,0:T(8,128)S(1)}, u32[]{:S(2)}, u32[]{:S(2)}) %all-to-all-start.1) | async-done | bytes 65568 | tf_op jit(solution)/shard_map/all_to_all | solution.py:184
  57.3 0.6 %reduce_max.9 = f32[]{:T(128)} reduce(f32[16,8,128]{2,1,0:T(8,128)S(1)} %all-to-all-done.1, f32[]{:T(128)} %constant.0.clone.1), dimensions={0,1,2}, to_apply=%region_0.0 | reduce | flops 16383 | bytes 65544 | tf_op jit(solution)/shard_map/reduce_max | solution.py:185
  58.6 0.0 collective-permute-done.3
  58.6 0.6 %divide_bitcast_fusion = f32[1,2,4096]{2,1,0:T(2,128)} fusion(f32[2,4096]{1,0:T(2,128)S(1)} %collective-permute-done.3, f32[]{:T(128)S(6)} %add.3), kind=kLoop, calls=%fused_computation | loop fusion | flops 8192 | bytes 65540 | tf_op jit(solution)/shard_map/broadcast_in_dim | solution.py:185
  (2 shorter events, 0.0 us)
Async XLA Ops:
  0.0 24.1 %copy-start.1 = (f32[1,2,4096]{2,1,0:T(2,128)S(1)}, f32[1,2,4096]{2,1,0:T(2,128)}, u32[]{:S(2)}) copy-start(f32[1,2,4096]{2,1,0:T(2,128)} %param.10) | copy-start | bytes 98308
  5.5 5.6 %collective-permute-start.1 = (f32[264,128]{1,0:T(8,128)}, f32[264,128]{1,0:T(8,128)S(1)}, u32[]{:S(2)}, u32[]{:S(2)}) collective-permute-start(f32[264,128]{1,0:T(8,128)} %products.1.m0_ref), channel_id=1, source_target_pairs={{0,16},{16,0},{1,17},{17,1},{2,18},{18,2},{3,19},{19,3},{4,20},{20... | collective-permute-start | bytes 405512 | tf_op jit(solution)/shard_map/ppermute | solution.py:158
  7.9 3.3 %collective-permute-start = (f32[264,128]{1,0:T(8,128)}, f32[264,128]{1,0:T(8,128)S(1)}, u32[]{:S(2)}, u32[]{:S(2)}) collective-permute-start(f32[264,128]{1,0:T(8,128)} %products.1.m0_ref), channel_id=1, source_target_pairs={{0,1},{1,0},{2,3},{3,2},{4,5},{5,4},{6,7},{7,6},{8,9},{9,8},{10,11... | collective-permute-start | bytes 405512 | tf_op jit(solution)/shard_map/ppermute | solution.py:159
  11.1 1.4 %collective-permute-start.2 = (f32[264,128]{1,0:T(8,128)S(1)}, f32[264,128]{1,0:T(8,128)S(1)}, u32[]{:S(2)}, u32[]{:S(2)}) collective-permute-start(f32[264,128]{1,0:T(8,128)S(1)} %collective-permute-done.1.m2_ref), channel_id=1, source_target_pairs={{0,1},{1,0},{2,3},{3,2},{4,5},{5,4},{6,7},{7,6},{8,9},{9,8},{10,11... | collective-permute-start | bytes 405512 | tf_op jit(solution)/shard_map/ppermute | solution.py:160
  12.5 0.9 %copy-start = (f32[264,128]{1,0:T(8,128)S(1)}, f32[264,128]{1,0:T(8,128)}, u32[]{:S(2)}) copy-start(f32[264,128]{1,0:T(8,128)} %products.1.m0_ref) | copy-start | bytes 405508
  15.5 21.5 %all-to-all-start = ((f32[8,64,128]{2,1,0:T(8,128)}), f32[8,64,128]{2,1,0:T(8,128)S(1)}, u32[]{:S(2)}, u32[]{:S(2)}) async-start(f32[8,64,128]{2,1,0:T(8,128)} %place.1), calls=%async_computation | async-start | bytes 524288 | tf_op jit(solution)/shard_map/all_to_all | solution.py:170
  37.5 1.3 %collective-permute-start.4 = (f32[8,128]{1,0:T(8,128)S(1)}, f32[8,128]{1,0:T(8,128)S(1)}, u32[]{:S(2)}, u32[]{:S(2)}) collective-permute-start(f32[8,128]{1,0:T(8,128)S(1)} %get-tuple-element.8), channel_id=1, source_target_pairs={{0,1},{1,0},{2,3},{3,2},{4,5},{5,4},{6,7},{7,6},{8,9},{9,8},{10,11... | collective-permute-start | bytes 12296 | tf_op jit(solution)/shard_map/ppermute | solution.py:182
  38.8 7.2 %collective-permute-start.5 = (f32[8,128]{1,0:T(8,128)S(1)}, f32[8,128]{1,0:T(8,128)S(1)}, u32[]{:S(2)}, u32[]{:S(2)}) collective-permute-start(f32[8,128]{1,0:T(8,128)S(1)} %max.3), channel_id=1, source_target_pairs={{0,32},{32,64},{64,96},{96,128},{128,160},{160,192},{192,224},{224... | collective-permute-start | bytes 12296 | tf_op jit(solution)/shard_map/ppermute | solution.py:183
  46.6 10.7 %all-to-all-start.1 = ((f32[16,8,128]{2,1,0:T(8,128)}), f32[16,8,128]{2,1,0:T(8,128)S(1)}, u32[]{:S(2)}, u32[]{:S(2)}) async-start(f32[16,8,128]{2,1,0:T(8,128)} %broadcast_in_dim.4), calls=%async_computation.1 | async-start | bytes 131072 | tf_op jit(solution)/shard_map/all_to_all | solution.py:184
  50.2 8.4 %collective-permute-start.3 = (f32[2,4096]{1,0:T(2,128)S(1)}, f32[2,4096]{1,0:T(2,128)S(1)}, u32[]{:S(2)}, u32[]{:S(2)}) collective-permute-start(f32[2,4096]{1,0:T(2,128)S(1)} %reshape.20), channel_id=1, source_target_pairs={{0,32},{32,64},{64,96},{96,128},{128,160},{160,192},{192,224},{224... | collective-permute-start | bytes 98312 | tf_op jit(solution)/shard_map/ppermute | solution.py:181

commit v3 on v2

--- a/solution.py
+++ b/solution.py
@@ -62,11 +62,16 @@
     for s in range(SECTORS - 1, -1, -1):
         first_ref[owner_ref[s]] = s
     small[3].wait()
+    slots = []
     for k in range(PAIRS):
         sector = out_ref[0, k]
         own = owner_ref[sector]
-        slot = (2 * own + jnp.where(first_ref[own] == sector, 0, 1)).astype(F32)
-        msg_ref[pl.ds(MSG + k, 1), :] = jnp.full((1, 2 * B), slot, F32)
+        slots.append((2 * own + jnp.where(first_ref[own] == sector, 0, 1)).astype(F32))
+    low_row = low_lanes((1, 2 * B))
+    for t in range(TILES):
+        a, b = slots[2 * t], slots[2 * t + 1]
+        msg_ref[pl.ds(MSG + 2 * t, 1), :] = jnp.where(low_row, a, b)
+        msg_ref[pl.ds(MSG + 2 * t + 1, 1), :] = jnp.where(low_row, b, a)
 
     for t in range(TILES):
         rows = pl.ds(t * 2 * B, 2 * B)
@@ -80,29 +85,23 @@
         msg_ref[pl.ds(t * B, B), :] = jnp.where(low, total[:B], total[B:])
 
 
-def place_kernel(m0_ref, m1_ref, m2_ref, m3_ref, out_ref, slots_ref, sem):
+def place_kernel(m0_ref, m1_ref, m2_ref, m3_ref, out_ref, turned_ref):
     refs = (m0_ref, m1_ref, m2_ref, m3_ref)
-    copies = [pltpu.make_async_copy(ref.at[pl.ds(MSG, PAIRS)], slots_ref.at[i], sem.at[i]) for i, ref in enumerate(refs)]
-    for copy in copies:
-        copy.start()
-    core, xl = lax.axis_index("core"), lax.axis_index("xl")
-    out_ref[...] = jnp.zeros_like(out_ref)
-    low = low_lanes((B, 2 * B))
-    half = jnp.where(low, 0, 1)
-    for copy in copies:
-        copy.wait()
     for i, ref in enumerate(refs):
-        for k in range(PAIRS):
-            slot = slots_ref[i, k, 0].astype(jnp.int32)
-            sec = slot >> 1
-
-            @pl.when(((sec & 1) == core) & ((sec >> 4) == xl))
-            def _(ref=ref, k=k, slot=slot, sec=sec):
-                tile = ref[pl.ds(k // 2 * B, B), :]
-                alone = jnp.where(low, tile, 0.0) if k % 2 == 0 else jnp.where(low, 0.0, tile)
-                spread = alone + pltpu.roll(alone, B, 1)
-                z = (sec >> 1) & (ZS - 1)
-                out_ref[z] = out_ref[z] + jnp.where(half == (slot & 1), spread, 0.0)
+        for t in range(TILES):
+            turned_ref[i, t] = pltpu.roll(ref[pl.ds(t * B, B), :], B, 1)
+    first = 2 * lax.axis_index("core") + 4 * ZS * lax.axis_index("xl")
+    half = jnp.where(low_lanes((1, 2 * B)), 0, 1)
+    for z in range(ZS):
+        slot = (first + 4 * z + half).astype(F32)
+        total = jnp.zeros((B, 2 * B), F32)
+        for i, ref in enumerate(refs):
+            for t in range(TILES):
+                straight = ref[pl.ds(MSG + 2 * t, 1), :] == slot
+                crossed = ref[pl.ds(MSG + 2 * t + 1, 1), :] == slot
+                total = total + jnp.where(straight, ref[pl.ds(t * B, B), :], 0.0)
+                total = total + jnp.where(crossed, turned_ref[i, t], 0.0)
+        out_ref[z] = total
 
 
 def project_kernel(parts_ref, projector_ref, out_ref, top_ref):
@@ -127,15 +126,34 @@
     top_ref[...] = top
 
 
+def finish_kernel(moved_ref, tops_ref, out_ref, rows_ref):
+    top = tops_ref[0]
+    for i in range(1, tops_ref.shape[0]):
+        top = jnp.maximum(top, tops_ref[i])
+    scale = jnp.max(top) + 1e-06
+    low = low_lanes((B // 2, 2 * B))
+    even = moved_ref[pl.ds(0, B // 2, stride=2), :] / scale
+    odd = moved_ref[pl.ds(1, B // 2, stride=2), :] / scale
+    rows_ref[0] = jnp.where(low, even, pltpu.roll(odd, B, 1))
+    rows_ref[1] = jnp.where(low, pltpu.roll(even, B, 1), odd)
+    for r in range(2):
+        for t in range(B // 2):
+            out_ref[pl.ds(r, 1), pl.ds(t * 2 * B, 2 * B)] = rows_ref[r, pl.ds(t, 1), :]
+
+
 VMEM = pl.BlockSpec(memory_space=pltpu.VMEM)
 ANY = pl.BlockSpec(memory_space=pl.ANY)
 SMALL = pltpu.CompilerParams(vmem_limit_bytes=8 << 20)
 
 
+def in_hbm(x):
+    return pltpu.with_memory_space_constraint(x, pltpu.HBM)
+
+
 def local(corner, edge, closing, projector, left_slot, out_sector, owner):
     message = pl.pallas_call(
         products_kernel,
-        out_shape=jax.ShapeDtypeStruct((MSG + PAIRS, 2 * B), F32),
+        out_shape=pltpu.VMEM((MSG + PAIRS, 2 * B), F32),
         in_specs=[ANY] * 6,
         out_specs=VMEM,
         scratch_shapes=[
@@ -152,37 +170,43 @@
             pltpu.SemaphoreType.DMA((TILES,)),
             pltpu.SemaphoreType.DMA((TILES,)),
         ],
-        compiler_params=pltpu.CompilerParams(vmem_limit_bytes=61 << 20),
+        compiler_params=pltpu.CompilerParams(vmem_limit_bytes=24 << 20),
         name="products",
-    )(left_slot, out_sector, owner, corner[0], edge.reshape(PAIRS * B, WIDE), closing.reshape(PAIRS * B, WIDE))
+    )(*map(in_hbm, (left_slot, out_sector, owner, corner[0], edge.reshape(PAIRS * B, WIDE), closing.reshape(PAIRS * B, WIDE))))
     over = lax.ppermute(message, "xl", SWAP)
     beside = lax.ppermute(message, "core", SWAP)
+    over, projector = lax.optimization_barrier((over, projector.reshape(2, B, B)))
     across = lax.ppermute(over, "core", SWAP)
     placed = pl.pallas_call(
         place_kernel,
-        out_shape=jax.ShapeDtypeStruct((ZS, B, 2 * B), F32),
+        out_shape=pltpu.VMEM((ZS, B, 2 * B), F32),
         in_specs=[VMEM] * 4,
         out_specs=VMEM,
-        scratch_shapes=[pltpu.SMEM((4, PAIRS, 2 * B), F32), pltpu.SemaphoreType.DMA((4,))],
+        scratch_shapes=[pltpu.VMEM((4, TILES, B, 2 * B), F32)],
         compiler_params=SMALL,
         name="place",
     )(message, beside, over, across)
     parts = lax.all_to_all(placed, "z", 0, 0)
     packed, top = pl.pallas_call(
         project_kernel,
-        out_shape=(jax.ShapeDtypeStruct((B, 2 * B), F32), jax.ShapeDtypeStruct((8, 2 * B), F32)),
+        out_shape=(pltpu.VMEM((B, 2 * B), F32), pltpu.VMEM((8, 2 * B), F32)),
         in_specs=[VMEM, VMEM],
         out_specs=(VMEM, VMEM),
         compiler_params=SMALL,
         name="project",
-    )(parts, projector.reshape(2, B, B))
-    ahead = [(i, (i + 1) % 8) for i in range(8)]
-    blocks = packed.reshape(B, 2, B).transpose(1, 0, 2).reshape(2, B * B)
-    moved = lax.ppermute(blocks, "col", ahead)
+    )(parts, projector)
     top = jnp.maximum(top, lax.ppermute(top, "core", SWAP))
-    top = lax.ppermute(top, "col", ahead)
-    tops = lax.all_to_all(jnp.broadcast_to(top[None], (2 * ZS, 8, 2 * B)), ("xl", "z"), 0, 0)
-    return (moved / (jnp.max(tops) + 1e-06))[None]
+    moved = lax.ppermute(jnp.concatenate([packed, top], axis=0), "col", [(i, (i + 1) % 8) for i in range(8)])
+    tops = lax.all_to_all(jnp.broadcast_to(moved[None, B:], (2 * ZS, 8, 2 * B)), ("xl", "z"), 0, 0)
+    return pl.pallas_call(
+        finish_kernel,
+        out_shape=jax.ShapeDtypeStruct((2, B * B), F32),
+        in_specs=[VMEM, VMEM],
+        out_specs=VMEM,
+        scratch_shapes=[pltpu.VMEM((2, B // 2, 2 * B), F32)],
+        compiler_params=SMALL,
+        name="finish",
+    )(moved, tops)[None]
 
 
 def solution(mesh):

time: 59.4 us -> 53.7 us (0.904)
  blocking collectives: 0 us -> 30.8 us
  waiting for transfers between devices: 30.4 us -> 10.9 us
  starting transfers between devices: 16.8 us -> 4.64 us
  local copies, waits for them, and re-layouts: 1.84 us -> 0.12 us
  other arithmetic: 1.25 us -> 0.01 us
  Pallas kernels: 8.13 us -> 7.01 us
  between operations: 0.72 us -> 0.04 us
    all_to_all x0 -> x2, blocking collectives: none -> 30.8 us  [the longest x1 20.5 us: local(): parts = lax.all_to_all(placed, 'z', 0, 0)]
    all_to_all x2 -> x0, waiting for transfers between devices: 19.7 us -> none  [the longest x1 12.7 us: local(): parts = lax.all_to_all(placed, 'z', 0, 0)]
    all_to_all x2 -> x0, starting transfers between devices: 12 us -> none  [the longest x1 8.62 us: local(): parts = lax.all_to_all(placed, 'z', 0, 0)]
    pallas_call x3 -> x4, Pallas kernels: 8.13 us -> 7.01 us  [the longest x1 4.87 us: local(): pl.pallas_call(products_kernel, out_shape=pltpu.VMEM((MSG + PAIRS, 2 * B)...]
    unnamed x4 -> x2, local copies, waits for them, and re-layouts: 0.91 us -> 0.01 us
    broadcast_in_dim x1 -> x0, other arithmetic: 0.63 us -> none  [local(): return (moved / (jnp.max(tops) + 1e-06))[None]]
    broadcast_in_dim x1, local copies, waits for them, and re-layouts: 0.63 us -> 0.01 us  [local(): jnp.broadcast_to(moved[None, B:], (2 * ZS, 8, 2 * B))]
    reduce_max x1 -> x0, other arithmetic: 0.61 us -> none  [local(): return (moved / (jnp.max(tops) + 1e-06))[None]]
  transfers between devices with their start and end apart: 8 -> 5, of which waited for: 6 -> 4; matrix products, arithmetic and copies ran while one was open for 2% -> 0% of each run, Pallas kernels for 0% -> 0%
where the time goes in v3:
time: 53.7 us; the launch traced here: 53.5 us
  blocking collectives  30.8 us (57%)
  waiting for transfers between devices  10.9 us (20%)
  Pallas kernels  7.01 us (13%)
  starting transfers between devices  4.64 us (9%)
    all_to_all x1, blocking collectives, local(): parts = lax.all_to_all(placed, 'z', 0, 0)  20.5 us
    all_to_all x1, blocking collectives, local(): lax.all_to_all(jnp.broadcast_to(moved[None, B:], (2 * ZS, 8, 2 * B)), ('x...  10.4 us
    ppermute x1, waiting for transfers between devices, local(): lax.ppermute(jnp.concatenate([packed, top], axis=0), 'col', [(i, (i + 1)...  5.45 us
    pallas_call x1, Pallas kernels, local(): pl.pallas_call(products_kernel, out_shape=pltpu.VMEM((MSG + PAIRS, 2 * B)...  4.87 us
    ppermute x1, waiting for transfers between devices, local(): over = lax.ppermute(message, 'xl', SWAP)  2.94 us
    ppermute x1, starting transfers between devices, local(): over = lax.ppermute(message, 'xl', SWAP)  2.36 us
    ppermute x1, starting transfers between devices, local(): lax.ppermute(jnp.concatenate([packed, top], axis=0), 'col', [(i, (i + 1)...  2.19 us
    ppermute x1, waiting for transfers between devices, local(): across = lax.ppermute(over, 'core', SWAP)  1.35 us
  transfers between devices with their start and end apart: 5, of which 4 were waited for; matrix products, arithmetic and copies ran while one was open for 0% of the time, Pallas kernels for 0%

profile of v3, /device:TPU:2, one launch (start us, length us, event | category | flops | bytes accessed | tf_op | source)
XLA Modules:
  0.0 53.5 jit_solution(4819571669591530588)
XLA Ops:
  0.0 0.0 copy-start
  0.0 4.9 %products.1.m0_ref = f32[264,128]{1,0:T(8,128)S(1)} custom-call(s32[1,8]{1,0:T(1,128)} %left_hbm.1, s32[1,8]{1,0:T(1,128)} %out_hbm.1, s32[64]{0:T(128)} %owner_hbm.1, bf16[2,4096]{1,0:T(2,128)(2,1)} %bitcast.6, bf16[512,4096]{1,0:T(8,128)(2,1)} %bitcast.4, bf16[512,4096]{1,0:T(8,128)(2,1)} %bitcast.5), custom_call_target="tpu_custom_call" | custom-call | tf_op jit(solution)/shard_map/products/pallas_call | solution.py:154
  4.9 2.4 %collective-permute-start.1 = (f32[264,128]{1,0:T(8,128)S(1)}, f32[264,128]{1,0:T(8,128)S(1)}, u32[]{:S(2)}, u32[]{:S(2)}) collective-permute-start(f32[264,128]{1,0:T(8,128)S(1)} %products.1.m0_ref), channel_id=1, source_target_pairs={{0,16},{16,0},{1,17},{17,1},{2,18},{18,2},{3,19},{19,3},{4,20},{20... | collective-permute-start | bytes 405512 | tf_op jit(solution)/shard_map/ppermute | solution.py:176
  7.2 0.0 collective-permute-start
  7.2 0.0 copy-done
  7.2 0.1 reshape.12.projector_ref
  7.4 2.9 %collective-permute-done.1.m2_ref = f32[264,128]{1,0:T(8,128)S(1)} collective-permute-done((f32[264,128]{1,0:T(8,128)S(1)}, f32[264,128]{1,0:T(8,128)S(1)}, u32[]{:S(2)}, u32[]{:S(2)}) %collective-permute-start.1) | collective-permute-done | bytes 135200 | tf_op jit(solution)/shard_map/ppermute | solution.py:176
  10.3 0.0 collective-permute-start.2
  10.3 0.0 collective-permute-done.m1_ref
  10.3 1.3 %collective-permute-done.2.m3_ref = f32[264,128]{1,0:T(8,128)S(1)} collective-permute-done((f32[264,128]{1,0:T(8,128)S(1)}, f32[264,128]{1,0:T(8,128)S(1)}, u32[]{:S(2)}, u32[]{:S(2)}) %collective-permute-start.2) | collective-permute-done | bytes 135200 | tf_op jit(solution)/shard_map/ppermute | solution.py:179
  11.6 0.8 %place.1 = f32[8,64,128]{2,1,0:T(8,128)S(1)} custom-call(f32[264,128]{1,0:T(8,128)S(1)} %products.1.m0_ref, f32[264,128]{1,0:T(8,128)S(1)} %collective-permute-done.m1_ref, f32[264,128]{1,0:T(8,128)S(1)} %collective-permute-done.1.m2_ref, f32[264,128]{1,0:T(8,128)S(1)} %collective-permute-done.2.m3_ref), custom_call_target="tpu_custom_call" | custom-call | tf_op jit(solution)/shard_map/place/pallas_call | solution.py:180
  12.4 20.5 %all_to_all.10.parts_ref = f32[8,64,128]{2,1,0:T(8,128)S(1)} all-to-all(f32[8,64,128]{2,1,0:T(8,128)S(1)} %place.1), channel_id=1, replica_groups=mesh['col'=8,'xl'=2,'z'=8,'core'=2] {'z'}, dimensions={0} | all-to-all | bytes 524288 | tf_op jit(solution)/shard_map/all_to_all | solution.py:189
  32.9 0.5 project.1
  33.4 0.1 collective-permute-start.3
  33.5 1.2 %collective-permute-done.3 = f32[8,128]{1,0:T(8,128)S(1)} collective-permute-done((f32[8,128]{1,0:T(8,128)S(1)}, f32[8,128]{1,0:T(8,128)S(1)}, u32[]{:S(2)}, u32[]{:S(2)}) %collective-permute-start.3) | collective-permute-done | bytes 4128 | tf_op jit(solution)/shard_map/ppermute | solution.py:198
  34.7 2.2 %collective-permute-start.4 = (f32[72,128]{1,0:T(8,128)S(1)}, f32[72,128]{1,0:T(8,128)S(1)}, u32[]{:S(2)}, u32[]{:S(2)}) collective-permute-start(f32[72,128]{1,0:T(8,128)S(1)} %pad_maximum_fusion), channel_id=1, source_target_pairs={{0,32},{32,64},{64,96},{96,128},{128,160},{160,192},{192,224},{224... | collective-permute-start | bytes 110600 | tf_op jit(solution)/shard_map/ppermute | solution.py:199
  36.9 5.5 %collective-permute-done.4.moved_ref = f32[72,128]{1,0:T(8,128)S(1)} collective-permute-done((f32[72,128]{1,0:T(8,128)S(1)}, f32[72,128]{1,0:T(8,128)S(1)}, u32[]{:S(2)}, u32[]{:S(2)}) %collective-permute-start.4) | collective-permute-done | bytes 36896 | tf_op jit(solution)/shard_map/ppermute | solution.py:199
  42.3 10.4 %all_to_all.11.tops_ref = f32[16,8,128]{2,1,0:T(8,128)S(1)} all-to-all(f32[16,8,128]{2,1,0:T(8,128)S(1)} %broadcast_in_dim.4), channel_id=1, replica_groups=mesh['col'=8,'xl'=2,'z'=8,'core'=2] {'xl','z'}, dimensions={0} | all-to-all | bytes 131072 | tf_op jit(solution)/shard_map/all_to_all | solution.py:200
  52.7 0.9 %finish.1 = f32[2,4096]{1,0:T(2,128)} custom-call(f32[72,128]{1,0:T(8,128)S(1)} %collective-permute-done.4.moved_ref, f32[16,8,128]{2,1,0:T(8,128)S(1)} %all_to_all.11.tops_ref), custom_call_target="tpu_custom_call" | custom-call | tf_op jit(solution)/shard_map/finish/pallas_call | solution.py:201
  (4 shorter events, 0.0 us)
Async XLA Ops:
  0.0 7.2 %copy-start = (f32[1,2,4096]{2,1,0:T(2,128)S(1)}, f32[1,2,4096]{2,1,0:T(2,128)}, u32[]{:S(2)}) copy-start(f32[1,2,4096]{2,1,0:T(2,128)} %param.10) | copy-start | bytes 98308
  4.9 5.4 %collective-permute-start.1 = (f32[264,128]{1,0:T(8,128)S(1)}, f32[264,128]{1,0:T(8,128)S(1)}, u32[]{:S(2)}, u32[]{:S(2)}) collective-permute-start(f32[264,128]{1,0:T(8,128)S(1)} %products.1.m0_ref), channel_id=1, source_target_pairs={{0,16},{16,0},{1,17},{17,1},{2,18},{18,2},{3,19},{19,3},{4,20},{20... | collective-permute-start | bytes 405512 | tf_op jit(solution)/shard_map/ppermute | solution.py:176
  7.2 3.1 %collective-permute-start = (f32[264,128]{1,0:T(8,128)S(1)}, f32[264,128]{1,0:T(8,128)S(1)}, u32[]{:S(2)}, u32[]{:S(2)}) collective-permute-start(f32[264,128]{1,0:T(8,128)S(1)} %products.1.m0_ref), channel_id=1, source_target_pairs={{0,1},{1,0},{2,3},{3,2},{4,5},{5,4},{6,7},{7,6},{8,9},{9,8},{10,11... | collective-permute-start | bytes 405512 | tf_op jit(solution)/shard_map/ppermute | solution.py:177
  10.3 1.4 %collective-permute-start.2 = (f32[264,128]{1,0:T(8,128)S(1)}, f32[264,128]{1,0:T(8,128)S(1)}, u32[]{:S(2)}, u32[]{:S(2)}) collective-permute-start(f32[264,128]{1,0:T(8,128)S(1)} %collective-permute-done.1.m2_ref), channel_id=1, source_target_pairs={{0,1},{1,0},{2,3},{3,2},{4,5},{5,4},{6,7},{7,6},{8,9},{9,8},{10,11... | collective-permute-start | bytes 405512 | tf_op jit(solution)/shard_map/ppermute | solution.py:179
  33.4 1.3 %collective-permute-start.3 = (f32[8,128]{1,0:T(8,128)S(1)}, f32[8,128]{1,0:T(8,128)S(1)}, u32[]{:S(2)}, u32[]{:S(2)}) collective-permute-start(f32[8,128]{1,0:T(8,128)S(1)} %get-tuple-element.12), channel_id=1, source_target_pairs={{0,1},{1,0},{2,3},{3,2},{4,5},{5,4},{6,7},{7,6},{8,9},{9,8},{10,11... | collective-permute-start | bytes 12296 | tf_op jit(solution)/shard_map/ppermute | solution.py:198
  34.7 7.6 %collective-permute-start.4 = (f32[72,128]{1,0:T(8,128)S(1)}, f32[72,128]{1,0:T(8,128)S(1)}, u32[]{:S(2)}, u32[]{:S(2)}) collective-permute-start(f32[72,128]{1,0:T(8,128)S(1)} %pad_maximum_fusion), channel_id=1, source_target_pairs={{0,32},{32,64},{64,96},{96,128},{128,160},{160,192},{192,224},{224... | collective-permute-start | bytes 110600 | tf_op jit(solution)/shard_map/ppermute | solution.py:199

commit v4 on v3

--- a/solution.py
+++ b/solution.py
@@ -85,15 +85,20 @@
         msg_ref[pl.ds(t * B, B), :] = jnp.where(low, total[:B], total[B:])
 
 
-def place_kernel(m0_ref, m1_ref, m2_ref, m3_ref, out_ref, turned_ref):
+HOPS = ((4, -3), (3, -2), (1, 2), (0, -1))
+
+
+def place_kernel(m0_ref, m1_ref, m2_ref, m3_ref, *rest):
+    out_refs, turned_ref = rest[:-1], rest[-1]
     refs = (m0_ref, m1_ref, m2_ref, m3_ref)
     for i, ref in enumerate(refs):
         for t in range(TILES):
             turned_ref[i, t] = pltpu.roll(ref[pl.ds(t * B, B), :], B, 1)
-    first = 2 * lax.axis_index("core") + 4 * ZS * lax.axis_index("xl")
-    half = jnp.where(low_lanes((1, 2 * B)), 0, 1)
-    for z in range(ZS):
-        slot = (first + 4 * z + half).astype(F32)
+    core, z = lax.axis_index("core"), lax.axis_index("z")
+    first = 4 * ZS * lax.axis_index("xl") + jnp.where(low_lanes((1, 2 * B)), 0, 1)
+
+    def placed(step, to):
+        slot = (first + 4 * ((z + step) & (ZS - 1)) + 2 * to).astype(F32)
         total = jnp.zeros((B, 2 * B), F32)
         for i, ref in enumerate(refs):
             for t in range(TILES):
@@ -101,29 +106,41 @@
                 crossed = ref[pl.ds(MSG + 2 * t + 1, 1), :] == slot
                 total = total + jnp.where(straight, ref[pl.ds(t * B, B), :], 0.0)
                 total = total + jnp.where(crossed, turned_ref[i, t], 0.0)
-        out_ref[z] = total
-
-
-def project_kernel(parts_ref, projector_ref, out_ref, top_ref):
-    joined = parts_ref[0]
-    for i in range(1, parts_ref.shape[0]):
-        joined = joined + parts_ref[i]
+        return total
+
+    for out_ref, (even, odd) in zip(out_refs, HOPS):
+        step = jnp.where(core == 0, even, odd)
+        out_ref[0] = placed(step, core)
+        out_ref[1] = placed(step, 1 - core)
+    out_refs[-1][...] = placed(0, core)
+
+
+def gather_kernel(*refs):
+    own_ref, out_ref = refs[-2:]
+    out_ref[0] = refs[0][0] + refs[1][0] + refs[2][0] + refs[3][0] + own_ref[...]
+    out_ref[1] = refs[0][1] + refs[1][1] + refs[2][1] + refs[3][1]
+
+
+def project_kernel(mine_ref, beside_ref, projector_ref, other_ref, out_ref):
     low = low_lanes((B, 2 * B))
-    beside = jnp.concatenate([projector_ref[0], projector_ref[1]], axis=1)
 
     def diagonal(packed):
         return jnp.concatenate([jnp.where(low, packed, 0.0), jnp.where(low, 0.0, packed)], axis=0)
 
-    proj = diagonal(beside)
-    inner = jnp.dot(diagonal(joined), proj, precision=lax.Precision.HIGHEST, preferred_element_type=F32)
-    full = lax.dot_general(proj, inner, (((0,), (0,)), ((), ())), precision=lax.Precision.HIGHEST, preferred_element_type=F32)
-    packed = jnp.where(low, full[:B], full[B:])
-    out_ref[...] = packed
-    size = jnp.abs(packed)
+    def project(joined, ref):
+        proj = diagonal(jnp.concatenate([ref[0], ref[1]], axis=1))
+        inner = jnp.dot(diagonal(joined), proj, precision=lax.Precision.HIGHEST, preferred_element_type=F32)
+        full = lax.dot_general(proj, inner, (((0,), (0,)), ((), ())), precision=lax.Precision.HIGHEST, preferred_element_type=F32)
+        return jnp.where(low, full[:B], full[B:])
+
+    packed = project(mine_ref[0] + beside_ref[1], projector_ref)
+    other = project(mine_ref[1] + beside_ref[0], other_ref)
+    out_ref[pl.ds(0, B), :] = packed
+    size = jnp.maximum(jnp.abs(packed), jnp.abs(other))
     top = size[:8]
     for i in range(1, 8):
         top = jnp.maximum(top, size[8 * i : 8 * i + 8])
-    top_ref[...] = top
+    out_ref[pl.ds(B, 8), :] = top
 
 
 def finish_kernel(moved_ref, tops_ref, out_ref, rows_ref):
@@ -175,28 +192,37 @@
     )(*map(in_hbm, (left_slot, out_sector, owner, corner[0], edge.reshape(PAIRS * B, WIDE), closing.reshape(PAIRS * B, WIDE))))
     over = lax.ppermute(message, "xl", SWAP)
     beside = lax.ppermute(message, "core", SWAP)
-    over, projector = lax.optimization_barrier((over, projector.reshape(2, B, B)))
+    projector = projector.reshape(2, B, B)
+    other = lax.ppermute(projector, "core", SWAP)
+    over, projector, other = lax.optimization_barrier((over, projector, other))
     across = lax.ppermute(over, "core", SWAP)
-    placed = pl.pallas_call(
+    tile, both = pltpu.VMEM((B, 2 * B), F32), pltpu.VMEM((2, B, 2 * B), F32)
+    *sent, own = pl.pallas_call(
         place_kernel,
-        out_shape=pltpu.VMEM((ZS, B, 2 * B), F32),
+        out_shape=[both] * len(HOPS) + [tile],
         in_specs=[VMEM] * 4,
-        out_specs=VMEM,
+        out_specs=[VMEM] * (len(HOPS) + 1),
         scratch_shapes=[pltpu.VMEM((4, TILES, B, 2 * B), F32)],
         compiler_params=SMALL,
         name="place",
     )(message, beside, over, across)
-    parts = lax.all_to_all(placed, "z", 0, 0)
-    packed, top = pl.pallas_call(
+
+    def along(x, steps):
+        moves = [(2 * z + q, 2 * ((z + steps[q]) % ZS) + q) for z in range(ZS) for q in range(2) if steps[q]]
+        return lax.ppermute(x, ("z", "core"), moves)
+
+    came = [along(x, steps) for x, steps in zip(sent, HOPS)]
+    mine = pl.pallas_call(gather_kernel, out_shape=both, in_specs=[VMEM] * (len(HOPS) + 1), out_specs=VMEM, compiler_params=SMALL, name="gather")(*came, own)
+    beside = lax.ppermute(mine, "core", SWAP)
+    payload = pl.pallas_call(
         project_kernel,
-        out_shape=(pltpu.VMEM((B, 2 * B), F32), pltpu.VMEM((8, 2 * B), F32)),
-        in_specs=[VMEM, VMEM],
-        out_specs=(VMEM, VMEM),
+        out_shape=pltpu.VMEM((B + 8, 2 * B), F32),
+        in_specs=[VMEM] * 4,
+        out_specs=VMEM,
         compiler_params=SMALL,
         name="project",
-    )(parts, projector)
-    top = jnp.maximum(top, lax.ppermute(top, "core", SWAP))
-    moved = lax.ppermute(jnp.concatenate([packed, top], axis=0), "col", [(i, (i + 1) % 8) for i in range(8)])
+    )(mine, beside, projector, other)
+    moved = lax.ppermute(payload, "col", [(i, (i + 1) % 8) for i in range(8)])
     tops = lax.all_to_all(jnp.broadcast_to(moved[None, B:], (2 * ZS, 8, 2 * B)), ("xl", "z"), 0, 0)
     return pl.pallas_call(
         finish_kernel,

time: 53.7 us -> 51.9 us (0.966)
  blocking collectives: 30.8 us -> 12.8 us
  starting transfers between devices: 4.64 us -> 15 us
  waiting for transfers between devices: 10.9 us -> 16.5 us
    all_to_all x1 -> x0, blocking collectives: 20.5 us -> none  [local(): parts = lax.all_to_all(placed, 'z', 0, 0)]
    ppermute x2 -> x7, starting transfers between devices: 2.28 us -> 12.2 us  [the longest x4 9.85 us: along(): return lax.ppermute(x, ('z', 'core'), moves)]
    ppermute x2 -> x7, waiting for transfers between devices: 6.6 us -> 13.4 us  [the longest x4 6.01 us: along(): return lax.ppermute(x, ('z', 'core'), moves)]
    all_to_all x1, blocking collectives: 10.4 us -> 12.8 us  [local(): lax.all_to_all(jnp.broadcast_to(moved[None, B:], (2 * ZS, 8, 2 * B)), ('x...]
    ppermute x1, waiting for transfers between devices: 2.94 us -> 1.66 us  [local(): over = lax.ppermute(message, 'xl', SWAP)]
    pallas_call x2 -> x3, Pallas kernels: 1.29 us -> 1.57 us  [the longest x1 0.92 us: local(): pl.pallas_call(place_kernel, out_shape=[both] * len(HOPS) + [tile], in_sp...]
  transfers between devices with their start and end apart: 5 -> 10, of which waited for: 4 -> 7; matrix products, arithmetic and copies ran while one was open for 0% -> 0% of each run, Pallas kernels for 0% -> 0%
where the time goes in v4:
time: 51.9 us; the launch traced here: 51.8 us
  waiting for transfers between devices  16.5 us (32%)
  starting transfers between devices  15 us (29%)
  blocking collectives  12.8 us (25%)
  Pallas kernels  7.29 us (14%)
    all_to_all x1, blocking collectives, local(): lax.all_to_all(jnp.broadcast_to(moved[None, B:], (2 * ZS, 8, 2 * B)), ('x...  12.8 us
    ppermute x4, starting transfers between devices, along(): return lax.ppermute(x, ('z', 'core'), moves)  9.85 us
    ppermute x4, waiting for transfers between devices, along(): return lax.ppermute(x, ('z', 'core'), moves)  6.01 us
    ppermute x1, waiting for transfers between devices, local(): moved = lax.ppermute(payload, 'col', [(i, (i + 1) % 8) for i in range(8)])  5.44 us
    pallas_call x1, Pallas kernels, local(): pl.pallas_call(products_kernel, out_shape=pltpu.VMEM((MSG + PAIRS, 2 * B)...  4.87 us
    ppermute x1, starting transfers between devices, local(): over = lax.ppermute(message, 'xl', SWAP)  2.36 us
    ppermute x1, starting transfers between devices, local(): moved = lax.ppermute(payload, 'col', [(i, (i + 1) % 8) for i in range(8)])  2.2 us
    ppermute x1, waiting for transfers between devices, local(): over = lax.ppermute(message, 'xl', SWAP)  1.66 us
  transfers between devices with their start and end apart: 10, of which 7 were waited for; matrix products, arithmetic and copies ran while one was open for 0% of the time, Pallas kernels for 0%

profile of v4, /device:TPU:2, one launch (start us, length us, event | category | flops | bytes accessed | tf_op | source)
XLA Modules:
  0.0 51.8 jit_solution(11139386455423976678)
XLA Ops:
  0.0 0.0 copy-start
  0.0 4.9 %products.1.m0_ref = f32[264,128]{1,0:T(8,128)S(1)} custom-call(s32[1,8]{1,0:T(1,128)} %left_hbm.1, s32[1,8]{1,0:T(1,128)} %out_hbm.1, s32[64]{0:T(128)} %owner_hbm.1, bf16[2,4096]{1,0:T(2,128)(2,1)} %bitcast.6, bf16[512,4096]{1,0:T(8,128)(2,1)} %bitcast.4, bf16[512,4096]{1,0:T(8,128)(2,1)} %bitcast.5), custom_call_target="tpu_custom_call" | custom-call | tf_op jit(solution)/shard_map/products/pallas_call | solution.py:171
  4.9 2.4 %collective-permute-start.1 = (f32[264,128]{1,0:T(8,128)S(1)}, f32[264,128]{1,0:T(8,128)S(1)}, u32[]{:S(2)}, u32[]{:S(2)}) collective-permute-start(f32[264,128]{1,0:T(8,128)S(1)} %products.1.m0_ref), channel_id=1, source_target_pairs={{0,16},{16,0},{1,17},{17,1},{2,18},{18,2},{3,19},{19,3},{4,20},{20... | collective-permute-start | bytes 405512 | tf_op jit(solution)/shard_map/ppermute | solution.py:193
  7.2 0.0 copy-done
  7.2 0.1 reshape.12.projector_ref
  7.3 0.0 collective-permute-start.2
  7.4 0.5 collective-permute-start
  7.9 0.7 %collective-permute-done.2.other_ref = f32[2,64,64]{2,1,0:T(8,128)S(1)} collective-permute-done((f32[2,64,64]{2,1,0:T(8,128)S(1)}, f32[2,64,64]{2,1,0:T(8,128)S(1)}, u32[]{:S(2)}, u32[]{:S(2)}) %collective-permute-start.2) | collective-permute-done | bytes 32800 | tf_op jit(solution)/shard_map/ppermute | solution.py:196
  8.6 1.7 %collective-permute-done.1.m2_ref = f32[264,128]{1,0:T(8,128)S(1)} collective-permute-done((f32[264,128]{1,0:T(8,128)S(1)}, f32[264,128]{1,0:T(8,128)S(1)}, u32[]{:S(2)}, u32[]{:S(2)}) %collective-permute-start.1) | collective-permute-done | bytes 135200 | tf_op jit(solution)/shard_map/ppermute | solution.py:193
  10.3 0.0 collective-permute-start.3
  10.3 0.0 collective-permute-done.m1_ref
  10.3 1.3 %collective-permute-done.3.m3_ref = f32[264,128]{1,0:T(8,128)S(1)} collective-permute-done((f32[264,128]{1,0:T(8,128)S(1)}, f32[264,128]{1,0:T(8,128)S(1)}, u32[]{:S(2)}, u32[]{:S(2)}) %collective-permute-start.3) | collective-permute-done | bytes 135200 | tf_op jit(solution)/shard_map/ppermute | solution.py:198
  11.6 0.9 %place.1 = (f32[2,64,128]{2,1,0:T(8,128)S(1)}, f32[2,64,128]{2,1,0:T(8,128)S(1)}, f32[2,64,128]{2,1,0:T(8,128)S(1)}, f32[2,64,128]{2,1,0:T(8,128)S(1)}, f32[64,128]{1,0:T(8,128)S(1)}) custom-call(f32[264,128]{1,0:T(8,128)S(1)} %products.1.m0_ref, f32[264,128]{1,0:T(8,128)S(1)} %collective-permute-done.m1_ref, f32[264,128]{1,0:T(8,128)S(1)} %collective-permute-done.1.m2_ref, ...), custom_call_target="tpu_custom_call" | custom-call | tf_op jit(solution)/shard_map/place/pallas_call | solution.py:200
  12.6 7.3 %collective-permute-start.4 = (f32[2,64,128]{2,1,0:T(8,128)S(1)}, f32[2,64,128]{2,1,0:T(8,128)S(1)}, u32[]{:S(2)}, u32[]{:S(2)}) collective-permute-start(f32[2,64,128]{2,1,0:T(8,128)S(1)} %get-tuple-element.14), channel_id=1, source_target_pairs={{0,8},{1,11},{2,10},{3,13},{4,12},{5,15},{6,14},{7,1},{8,0},{9,3},... | collective-permute-start | bytes 196616 | tf_op jit(solution)/shard_map/ppermute | solution.py:212
  19.8 1.9 %collective-permute-start.5 = (f32[2,64,128]{2,1,0:T(8,128)S(1)}, f32[2,64,128]{2,1,0:T(8,128)S(1)}, u32[]{:S(2)}, u32[]{:S(2)}) collective-permute-start(f32[2,64,128]{2,1,0:T(8,128)S(1)} %get-tuple-element.15), channel_id=1, source_target_pairs={{0,6},{1,13},{2,8},{3,15},{4,10},{5,1},{6,12},{7,3},{8,14},{9,5},{... | collective-permute-start | bytes 196616 | tf_op jit(solution)/shard_map/ppermute | solution.py:212
  21.8 0.0 collective-permute-start.6
  21.8 0.7 %collective-permute-start.7 = (f32[2,64,128]{2,1,0:T(8,128)S(1)}, f32[2,64,128]{2,1,0:T(8,128)S(1)}, u32[]{:S(2)}, u32[]{:S(2)}) collective-permute-start(f32[2,64,128]{2,1,0:T(8,128)S(1)} %get-tuple-element.17), channel_id=1, source_target_pairs={{1,15},{3,1},{5,3},{7,5},{9,7},{11,9},{13,11},{15,13},{17,31},{19,... | collective-permute-start | bytes 196616 | tf_op jit(solution)/shard_map/ppermute | solution.py:212
  22.4 0.0 collective-permute-done.4.refs_0_
  22.4 5.8 %collective-permute-done.5.refs_1_ = f32[2,64,128]{2,1,0:T(8,128)S(1)} collective-permute-done((f32[2,64,128]{2,1,0:T(8,128)S(1)}, f32[2,64,128]{2,1,0:T(8,128)S(1)}, u32[]{:S(2)}, u32[]{:S(2)}) %collective-permute-start.5) | collective-permute-done | bytes 65568 | tf_op jit(solution)/shard_map/ppermute | solution.py:212
  28.2 0.2 collective-permute-done.6.refs_2_
  28.5 0.0 collective-permute-done.7.refs_3_
  28.5 0.1 collective-permute-start.8
  28.6 1.2 %collective-permute-done.8.beside_ref = f32[2,64,128]{2,1,0:T(8,128)S(1)} collective-permute-done((f32[2,64,128]{2,1,0:T(8,128)S(1)}, f32[2,64,128]{2,1,0:T(8,128)S(1)}, u32[]{:S(2)}, u32[]{:S(2)}) %collective-permute-start.8) | collective-permute-done | bytes 65568 | tf_op jit(solution)/shard_map/ppermute | solution.py:216
  29.8 0.6 %project.1 = f32[72,128]{1,0:T(8,128)S(1)} custom-call(f32[2,64,128]{2,1,0:T(8,128)S(1)} %gather.1.mine_ref, f32[2,64,128]{2,1,0:T(8,128)S(1)} %collective-permute-done.8.beside_ref, f32[2,64,64]{2,1,0:T(8,128)S(1)} %reshape.12.projector_ref, f32[2,64,64]{2,1,0:T(8,128)S(1)} %collective-permute-done.2.other_ref), custom_call_target="tpu_custom_call" | custom-call | tf_op jit(solution)/shard_map/project/pallas_call | solution.py:217
  30.5 2.2 %collective-permute-start.9 = (f32[72,128]{1,0:T(8,128)S(1)}, f32[72,128]{1,0:T(8,128)S(1)}, u32[]{:S(2)}, u32[]{:S(2)}) collective-permute-start(f32[72,128]{1,0:T(8,128)S(1)} %project.1), channel_id=1, source_target_pairs={{0,32},{32,64},{64,96},{96,128},{128,160},{160,192},{192,224},{224... | collective-permute-start | bytes 110600 | tf_op jit(solution)/shard_map/ppermute | solution.py:225
  32.7 5.4 %collective-permute-done.9.moved_ref = f32[72,128]{1,0:T(8,128)S(1)} collective-permute-done((f32[72,128]{1,0:T(8,128)S(1)}, f32[72,128]{1,0:T(8,128)S(1)}, u32[]{:S(2)}, u32[]{:S(2)}) %collective-permute-start.9) | collective-permute-done | bytes 36896 | tf_op jit(solution)/shard_map/ppermute | solution.py:225
  38.1 12.8 %all_to_all.5.tops_ref = f32[16,8,128]{2,1,0:T(8,128)S(1)} all-to-all(f32[16,8,128]{2,1,0:T(8,128)S(1)} %broadcast_in_dim.4), channel_id=1, replica_groups=mesh['col'=8,'xl'=2,'z'=8,'core'=2] {'xl','z'}, dimensions={0} | all-to-all | bytes 131072 | tf_op jit(solution)/shard_map/all_to_all | solution.py:226
  50.9 0.9 %finish.1 = f32[2,4096]{1,0:T(2,128)} custom-call(f32[72,128]{1,0:T(8,128)S(1)} %collective-permute-done.9.moved_ref, f32[16,8,128]{2,1,0:T(8,128)S(1)} %all_to_all.5.tops_ref), custom_call_target="tpu_custom_call" | custom-call | tf_op jit(solution)/shard_map/finish/pallas_call | solution.py:227
  (3 shorter events, 0.0 us)
Async XLA Ops:
  0.0 7.2 %copy-start = (f32[1,2,4096]{2,1,0:T(2,128)S(1)}, f32[1,2,4096]{2,1,0:T(2,128)}, u32[]{:S(2)}) copy-start(f32[1,2,4096]{2,1,0:T(2,128)} %param.10) | copy-start | bytes 98308
  4.9 5.4 %collective-permute-start.1 = (f32[264,128]{1,0:T(8,128)S(1)}, f32[264,128]{1,0:T(8,128)S(1)}, u32[]{:S(2)}, u32[]{:S(2)}) collective-permute-start(f32[264,128]{1,0:T(8,128)S(1)} %products.1.m0_ref), channel_id=1, source_target_pairs={{0,16},{16,0},{1,17},{17,1},{2,18},{18,2},{3,19},{19,3},{4,20},{20... | collective-permute-start | bytes 405512 | tf_op jit(solution)/shard_map/ppermute | solution.py:193
  7.3 1.3 %collective-permute-start.2 = (f32[2,64,64]{2,1,0:T(8,128)S(1)}, f32[2,64,64]{2,1,0:T(8,128)S(1)}, u32[]{:S(2)}, u32[]{:S(2)}) collective-permute-start(f32[2,64,64]{2,1,0:T(8,128)S(1)} %reshape.12.projector_ref), channel_id=1, source_target_pairs={{0,1},{1,0},{2,3},{3,2},{4,5},{5,4},{6,7},{7,6},{8,9},{9,8},{10,11... | collective-permute-start | bytes 98312 | tf_op jit(solution)/shard_map/ppermute | solution.py:196
  7.4 2.9 %collective-permute-start = (f32[264,128]{1,0:T(8,128)S(1)}, f32[264,128]{1,0:T(8,128)S(1)}, u32[]{:S(2)}, u32[]{:S(2)}) collective-permute-start(f32[264,128]{1,0:T(8,128)S(1)} %products.1.m0_ref), channel_id=1, source_target_pairs={{0,1},{1,0},{2,3},{3,2},{4,5},{5,4},{6,7},{7,6},{8,9},{9,8},{10,11... | collective-permute-start | bytes 405512 | tf_op jit(solution)/shard_map/ppermute | solution.py:194
  10.3 1.4 %collective-permute-start.3 = (f32[264,128]{1,0:T(8,128)S(1)}, f32[264,128]{1,0:T(8,128)S(1)}, u32[]{:S(2)}, u32[]{:S(2)}) collective-permute-start(f32[264,128]{1,0:T(8,128)S(1)} %collective-permute-done.1.m2_ref), channel_id=1, source_target_pairs={{0,1},{1,0},{2,3},{3,2},{4,5},{5,4},{6,7},{7,6},{8,9},{9,8},{10,11... | collective-permute-start | bytes 405512 | tf_op jit(solution)/shard_map/ppermute | solution.py:198
  12.6 9.9 %collective-permute-start.4 = (f32[2,64,128]{2,1,0:T(8,128)S(1)}, f32[2,64,128]{2,1,0:T(8,128)S(1)}, u32[]{:S(2)}, u32[]{:S(2)}) collective-permute-start(f32[2,64,128]{2,1,0:T(8,128)S(1)} %get-tuple-element.14), channel_id=1, source_target_pairs={{0,8},{1,11},{2,10},{3,13},{4,12},{5,15},{6,14},{7,1},{8,0},{9,3},... | collective-permute-start | bytes 196616 | tf_op jit(solution)/shard_map/ppermute | solution.py:212
  19.8 8.4 %collective-permute-start.5 = (f32[2,64,128]{2,1,0:T(8,128)S(1)}, f32[2,64,128]{2,1,0:T(8,128)S(1)}, u32[]{:S(2)}, u32[]{:S(2)}) collective-permute-start(f32[2,64,128]{2,1,0:T(8,128)S(1)} %get-tuple-element.15), channel_id=1, source_target_pairs={{0,6},{1,13},{2,8},{3,15},{4,10},{5,1},{6,12},{7,3},{8,14},{9,5},{... | collective-permute-start | bytes 196616 | tf_op jit(solution)/shard_map/ppermute | solution.py:212
  21.8 6.7 %collective-permute-start.6 = (f32[2,64,128]{2,1,0:T(8,128)S(1)}, f32[2,64,128]{2,1,0:T(8,128)S(1)}, u32[]{:S(2)}, u32[]{:S(2)}) collective-permute-start(f32[2,64,128]{2,1,0:T(8,128)S(1)} %get-tuple-element.16), channel_id=1, source_target_pairs={{0,2},{1,5},{2,4},{3,7},{4,6},{5,9},{6,8},{7,11},{8,10},{9,13},{10... | collective-permute-start | bytes 196616 | tf_op jit(solution)/shard_map/ppermute | solution.py:212
  21.8 6.7 %collective-permute-start.7 = (f32[2,64,128]{2,1,0:T(8,128)S(1)}, f32[2,64,128]{2,1,0:T(8,128)S(1)}, u32[]{:S(2)}, u32[]{:S(2)}) collective-permute-start(f32[2,64,128]{2,1,0:T(8,128)S(1)} %get-tuple-element.17), channel_id=1, source_target_pairs={{1,15},{3,1},{5,3},{7,5},{9,7},{11,9},{13,11},{15,13},{17,31},{19,... | collective-permute-start | bytes 196616 | tf_op jit(solution)/shard_map/ppermute | solution.py:212
  28.5 1.3 %collective-permute-start.8 = (f32[2,64,128]{2,1,0:T(8,128)S(1)}, f32[2,64,128]{2,1,0:T(8,128)S(1)}, u32[]{:S(2)}, u32[]{:S(2)}) collective-permute-start(f32[2,64,128]{2,1,0:T(8,128)S(1)} %gather.1.mine_ref), channel_id=1, source_target_pairs={{0,1},{1,0},{2,3},{3,2},{4,5},{5,4},{6,7},{7,6},{8,9},{9,8},{10,11... | collective-permute-start | bytes 196616 | tf_op jit(solution)/shard_map/ppermute | solution.py:216
  30.5 7.6 %collective-permute-start.9 = (f32[72,128]{1,0:T(8,128)S(1)}, f32[72,128]{1,0:T(8,128)S(1)}, u32[]{:S(2)}, u32[]{:S(2)}) collective-permute-start(f32[72,128]{1,0:T(8,128)S(1)} %project.1), channel_id=1, source_target_pairs={{0,32},{32,64},{64,96},{96,128},{128,160},{160,192},{192,224},{224... | collective-permute-start | bytes 110600 | tf_op jit(solution)/shard_map/ppermute | solution.py:225

commit v5 on v4

--- a/solution.py
+++ b/solution.py
@@ -1,3 +1,5 @@
+import functools
+
 import jax
 import jax.numpy as jnp
 from jax import lax
@@ -88,18 +90,19 @@
 HOPS = ((4, -3), (3, -2), (1, 2), (0, -1))
 
 
-def place_kernel(m0_ref, m1_ref, m2_ref, m3_ref, *rest):
-    out_refs, turned_ref = rest[:-1], rest[-1]
-    refs = (m0_ref, m1_ref, m2_ref, m3_ref)
+def place_kernel(count, before, *all_refs):
+    refs, all_refs = all_refs[:count], all_refs[count:]
+    outs = len(HOPS) + 1
+    before_refs, all_refs = all_refs[: outs * before], all_refs[outs * before :]
+    out_refs, turned_ref = all_refs[:-1], all_refs[-1]
     for i, ref in enumerate(refs):
         for t in range(TILES):
             turned_ref[i, t] = pltpu.roll(ref[pl.ds(t * B, B), :], B, 1)
     core, z = lax.axis_index("core"), lax.axis_index("z")
     first = 4 * ZS * lax.axis_index("xl") + jnp.where(low_lanes((1, 2 * B)), 0, 1)
 
-    def placed(step, to):
+    def placed(step, to, total):
         slot = (first + 4 * ((z + step) & (ZS - 1)) + 2 * to).astype(F32)
-        total = jnp.zeros((B, 2 * B), F32)
         for i, ref in enumerate(refs):
             for t in range(TILES):
                 straight = ref[pl.ds(MSG + 2 * t, 1), :] == slot
@@ -108,11 +111,12 @@
                 total = total + jnp.where(crossed, turned_ref[i, t], 0.0)
         return total
 
-    for out_ref, (even, odd) in zip(out_refs, HOPS):
+    zero = jnp.zeros((B, 2 * B), F32)
+    for n, (even, odd) in enumerate(HOPS):
         step = jnp.where(core == 0, even, odd)
-        out_ref[0] = placed(step, core)
-        out_ref[1] = placed(step, 1 - core)
-    out_refs[-1][...] = placed(0, core)
+        out_refs[n][0] = placed(step, core, before_refs[n][0] if before else zero)
+        out_refs[n][1] = placed(step, 1 - core, before_refs[n][1] if before else zero)
+    out_refs[-1][...] = placed(0, core, before_refs[-1][...] if before else zero)
 
 
 def gather_kernel(*refs):
@@ -140,14 +144,11 @@
     top = size[:8]
     for i in range(1, 8):
         top = jnp.maximum(top, size[8 * i : 8 * i + 8])
-    out_ref[pl.ds(B, 8), :] = top
+    out_ref[pl.ds(B, 2 * ZS), :] = jnp.broadcast_to(jnp.max(top, axis=0, keepdims=True), (2 * ZS, 2 * B))
 
 
 def finish_kernel(moved_ref, tops_ref, out_ref, rows_ref):
-    top = tops_ref[0]
-    for i in range(1, tops_ref.shape[0]):
-        top = jnp.maximum(top, tops_ref[i])
-    scale = jnp.max(top) + 1e-06
+    scale = jnp.max(tops_ref[...]) + 1e-06
     low = low_lanes((B // 2, 2 * B))
     even = moved_ref[pl.ds(0, B // 2, stride=2), :] / scale
     odd = moved_ref[pl.ds(1, B // 2, stride=2), :] / scale
@@ -161,6 +162,20 @@
 VMEM = pl.BlockSpec(memory_space=pltpu.VMEM)
 ANY = pl.BlockSpec(memory_space=pl.ANY)
 SMALL = pltpu.CompilerParams(vmem_limit_bytes=8 << 20)
+
+
+def place(messages, before=()):
+    tile, both = pltpu.VMEM((B, 2 * B), F32), pltpu.VMEM((2, B, 2 * B), F32)
+    outs = len(HOPS) + 1
+    return pl.pallas_call(
+        functools.partial(place_kernel, len(messages), bool(before)),
+        out_shape=[both] * len(HOPS) + [tile],
+        in_specs=[VMEM] * (len(messages) + len(before)),
+        out_specs=[VMEM] * outs,
+        scratch_shapes=[pltpu.VMEM((len(messages), TILES, B, 2 * B), F32)],
+        compiler_params=SMALL,
+        name="place",
+    )(*messages, *before)
 
 
 def in_hbm(x):
@@ -196,16 +211,10 @@
     other = lax.ppermute(projector, "core", SWAP)
     over, projector, other = lax.optimization_barrier((over, projector, other))
     across = lax.ppermute(over, "core", SWAP)
-    tile, both = pltpu.VMEM((B, 2 * B), F32), pltpu.VMEM((2, B, 2 * B), F32)
-    *sent, own = pl.pallas_call(
-        place_kernel,
-        out_shape=[both] * len(HOPS) + [tile],
-        in_specs=[VMEM] * 4,
-        out_specs=[VMEM] * (len(HOPS) + 1),
-        scratch_shapes=[pltpu.VMEM((4, TILES, B, 2 * B), F32)],
-        compiler_params=SMALL,
-        name="place",
-    )(message, beside, over, across)
+    parts = place((message, beside))
+    parts = place((over,), parts)
+    *sent, own = place((across,), parts)
+    both = pltpu.VMEM((2, B, 2 * B), F32)
 
     def along(x, steps):
         moves = [(2 * z + q, 2 * ((z + steps[q]) % ZS) + q) for z in range(ZS) for q in range(2) if steps[q]]
@@ -216,14 +225,14 @@
     beside = lax.ppermute(mine, "core", SWAP)
     payload = pl.pallas_call(
         project_kernel,
-        out_shape=pltpu.VMEM((B + 8, 2 * B), F32),
+        out_shape=pltpu.VMEM((B + 2 * ZS, 2 * B), F32),
         in_specs=[VMEM] * 4,
         out_specs=VMEM,
         compiler_params=SMALL,
         name="project",
     )(mine, beside, projector, other)
     moved = lax.ppermute(payload, "col", [(i, (i + 1) % 8) for i in range(8)])
-    tops = lax.all_to_all(jnp.broadcast_to(moved[None, B:], (2 * ZS, 8, 2 * B)), ("xl", "z"), 0, 0)
+    tops = lax.all_to_all(moved[B:], ("xl", "z"), 0, 0, tiled=True)
     return pl.pallas_call(
         finish_kernel,
         out_shape=jax.ShapeDtypeStruct((2, B * B), F32),

time: 51.9 us -> 51 us (0.983)
  waiting for transfers between devices: 16.5 us -> 15.8 us
    ppermute x1, waiting for transfers between devices: 1.35 us -> 0.62 us  [local(): across = lax.ppermute(over, 'core', SWAP)]
    pallas_call x2 -> x4, Pallas kernels: 1.55 us -> 1.6 us  [the longest x3 0.97 us: place(): pl.pallas_call(functools.partial(place_kernel, len(messages), bool(before...]
  transfers between devices with their start and end apart: 10 -> 10, of which waited for: 7 -> 7; matrix products, arithmetic and copies ran while one was open for 0% -> 0% of each run, Pallas kernels for 0% -> 1%
where the time goes in v5:
time: 51 us; the launch traced here: 50.9 us
  waiting for transfers between devices  15.8 us (31%)
  starting transfers between devices  15 us (29%)
  blocking collectives  12.6 us (25%)
  Pallas kernels  7.33 us (14%)
    all_to_all x1, blocking collectives, local(): tops = lax.all_to_all(moved[B:], ('xl', 'z'), 0, 0, tiled=True)  12.6 us
    ppermute x4, starting transfers between devices, along(): return lax.ppermute(x, ('z', 'core'), moves)  9.85 us
    ppermute x4, waiting for transfers between devices, along(): return lax.ppermute(x, ('z', 'core'), moves)  6.01 us
    ppermute x1, waiting for transfers between devices, local(): moved = lax.ppermute(payload, 'col', [(i, (i + 1) % 8) for i in range(8)])  5.49 us
    pallas_call x1, Pallas kernels, local(): pl.pallas_call(products_kernel, out_shape=pltpu.VMEM((MSG + PAIRS, 2 * B)...  4.87 us
    ppermute x1, starting transfers between devices, local(): over = lax.ppermute(message, 'xl', SWAP)  2.36 us
    ppermute x1, starting transfers between devices, local(): moved = lax.ppermute(payload, 'col', [(i, (i + 1) % 8) for i in range(8)])  2.21 us
    ppermute x1, waiting for transfers between devices, local(): over = lax.ppermute(message, 'xl', SWAP)  1.66 us
  transfers between devices with their start and end apart: 10, of which 7 were waited for; matrix products, arithmetic and copies ran while one was open for 0% of the time, Pallas kernels for 1%

profile of v5, /device:TPU:2, one launch (start us, length us, event | category | flops | bytes accessed | tf_op | source)
XLA Modules:
  0.0 50.9 jit_solution(13351791382800302476)
XLA Ops:
  0.0 0.0 copy-start
  0.0 4.9 %products.1.all_refs_0_ = f32[264,128]{1,0:T(8,128)S(1)} custom-call(s32[1,8]{1,0:T(1,128)} %left_hbm.1, s32[1,8]{1,0:T(1,128)} %out_hbm.1, s32[64]{0:T(128)} %owner_hbm.1, bf16[2,4096]{1,0:T(2,128)(2,1)} %bitcast.12, bf16[512,4096]{1,0:T(8,128)(2,1)} %bitcast.9, bf16[512,4096]{1,0:T(8,128)(2,1)} %bitcast.10), custom_call_target="tpu_custom_call" | custom-call | tf_op jit(solution)/shard_map/products/pallas_call | solution.py:186
  4.9 2.4 %collective-permute-start = (f32[264,128]{1,0:T(8,128)S(1)}, f32[264,128]{1,0:T(8,128)S(1)}, u32[]{:S(2)}, u32[]{:S(2)}) collective-permute-start(f32[264,128]{1,0:T(8,128)S(1)} %products.1.all_refs_0_), channel_id=1, source_target_pairs={{0,16},{16,0},{1,17},{17,1},{2,18},{18,2},{3,19},{19,3},{4,20},{20... | collective-permute-start | bytes 405512 | tf_op jit(solution)/shard_map/ppermute | solution.py:208
  7.2 0.0 copy-done
  7.2 0.1 reshape.13.projector_ref
  7.3 0.0 collective-permute-start.1
  7.4 0.5 collective-permute-start.3
  7.9 0.7 %collective-permute-done.1.other_ref = f32[2,64,64]{2,1,0:T(8,128)S(1)} collective-permute-done((f32[2,64,64]{2,1,0:T(8,128)S(1)}, f32[2,64,64]{2,1,0:T(8,128)S(1)}, u32[]{:S(2)}, u32[]{:S(2)}) %collective-permute-start.1) | collective-permute-done | bytes 32800 | tf_op jit(solution)/shard_map/ppermute | solution.py:211
  8.6 1.7 %collective-permute-done.all_refs_0_ = f32[264,128]{1,0:T(8,128)S(1)} collective-permute-done((f32[264,128]{1,0:T(8,128)S(1)}, f32[264,128]{1,0:T(8,128)S(1)}, u32[]{:S(2)}, u32[]{:S(2)}) %collective-permute-start) | collective-permute-done | bytes 135200 | tf_op jit(solution)/shard_map/ppermute | solution.py:208
  10.3 0.0 collective-permute-start.2
  10.3 0.0 collective-permute-done.3.all_refs_1_
  10.3 0.5 place.3
  10.8 0.3 place.4
  11.0 0.6 %collective-permute-done.2.all_refs_0_ = f32[264,128]{1,0:T(8,128)S(1)} collective-permute-done((f32[264,128]{1,0:T(8,128)S(1)}, f32[264,128]{1,0:T(8,128)S(1)}, u32[]{:S(2)}, u32[]{:S(2)}) %collective-permute-start.2) | collective-permute-done | bytes 135200 | tf_op jit(solution)/shard_map/ppermute | solution.py:213
  11.6 0.2 place.5
  11.9 7.3 %collective-permute-start.4 = (f32[2,64,128]{2,1,0:T(8,128)S(1)}, f32[2,64,128]{2,1,0:T(8,128)S(1)}, u32[]{:S(2)}, u32[]{:S(2)}) collective-permute-start(f32[2,64,128]{2,1,0:T(8,128)S(1)} %get-tuple-element.34), channel_id=1, source_target_pairs={{0,8},{1,11},{2,10},{3,13},{4,12},{5,15},{6,14},{7,1},{8,0},{9,3},... | collective-permute-start | bytes 196616 | tf_op jit(solution)/shard_map/ppermute | solution.py:221
  19.2 1.9 %collective-permute-start.5 = (f32[2,64,128]{2,1,0:T(8,128)S(1)}, f32[2,64,128]{2,1,0:T(8,128)S(1)}, u32[]{:S(2)}, u32[]{:S(2)}) collective-permute-start(f32[2,64,128]{2,1,0:T(8,128)S(1)} %get-tuple-element.35), channel_id=1, source_target_pairs={{0,6},{1,13},{2,8},{3,15},{4,10},{5,1},{6,12},{7,3},{8,14},{9,5},{... | collective-permute-start | bytes 196616 | tf_op jit(solution)/shard_map/ppermute | solution.py:221
  21.1 0.0 collective-permute-start.6
  21.1 0.7 %collective-permute-start.7 = (f32[2,64,128]{2,1,0:T(8,128)S(1)}, f32[2,64,128]{2,1,0:T(8,128)S(1)}, u32[]{:S(2)}, u32[]{:S(2)}) collective-permute-start(f32[2,64,128]{2,1,0:T(8,128)S(1)} %get-tuple-element.37), channel_id=1, source_target_pairs={{1,15},{3,1},{5,3},{7,5},{9,7},{11,9},{13,11},{15,13},{17,31},{19,... | collective-permute-start | bytes 196616 | tf_op jit(solution)/shard_map/ppermute | solution.py:221
  21.8 0.0 collective-permute-done.4.refs_0_
  21.8 5.8 %collective-permute-done.5.refs_1_ = f32[2,64,128]{2,1,0:T(8,128)S(1)} collective-permute-done((f32[2,64,128]{2,1,0:T(8,128)S(1)}, f32[2,64,128]{2,1,0:T(8,128)S(1)}, u32[]{:S(2)}, u32[]{:S(2)}) %collective-permute-start.5) | collective-permute-done | bytes 65568 | tf_op jit(solution)/shard_map/ppermute | solution.py:221
  27.5 0.2 collective-permute-done.6.refs_2_
  27.8 0.0 collective-permute-done.7.refs_3_
  27.8 0.1 collective-permute-start.8
  27.9 1.2 %collective-permute-done.8.beside_ref = f32[2,64,128]{2,1,0:T(8,128)S(1)} collective-permute-done((f32[2,64,128]{2,1,0:T(8,128)S(1)}, f32[2,64,128]{2,1,0:T(8,128)S(1)}, u32[]{:S(2)}, u32[]{:S(2)}) %collective-permute-start.8) | collective-permute-done | bytes 65568 | tf_op jit(solution)/shard_map/ppermute | solution.py:225
  29.1 0.6 %project.1 = f32[80,128]{1,0:T(8,128)S(1)} custom-call(f32[2,64,128]{2,1,0:T(8,128)S(1)} %gather.1.mine_ref, f32[2,64,128]{2,1,0:T(8,128)S(1)} %collective-permute-done.8.beside_ref, f32[2,64,64]{2,1,0:T(8,128)S(1)} %reshape.13.projector_ref, f32[2,64,64]{2,1,0:T(8,128)S(1)} %collective-permute-done.1.other_ref), custom_call_target="tpu_custom_call" | custom-call | tf_op jit(solution)/shard_map/project/pallas_call | solution.py:226
  29.8 2.2 %collective-permute-start.9 = (f32[80,128]{1,0:T(8,128)S(1)}, f32[80,128]{1,0:T(8,128)S(1)}, u32[]{:S(2)}, u32[]{:S(2)}) collective-permute-start(f32[80,128]{1,0:T(8,128)S(1)} %project.1), channel_id=1, source_target_pairs={{0,32},{32,64},{64,96},{96,128},{128,160},{160,192},{192,224},{224... | collective-permute-start | bytes 122888 | tf_op jit(solution)/shard_map/ppermute | solution.py:234
  32.0 5.5 %collective-permute-done.9.moved_ref = f32[80,128]{1,0:T(8,128)S(1)} collective-permute-done((f32[80,128]{1,0:T(8,128)S(1)}, f32[80,128]{1,0:T(8,128)S(1)}, u32[]{:S(2)}, u32[]{:S(2)}) %collective-permute-start.9) | collective-permute-done | bytes 40992 | tf_op jit(solution)/shard_map/ppermute | solution.py:234
  37.5 12.6 %all_to_all.11 = f32[16,1,128]{2,1,0:T(1,128)S(1)} all-to-all(f32[16,1,128]{2,1,0:T(1,128)S(1)} %bitcast.11), channel_id=1, replica_groups=mesh['col'=8,'xl'=2,'z'=8,'core'=2] {'xl','z'}, dimensions={0} | all-to-all | bytes 16384 | tf_op jit(solution)/shard_map/all_to_all | solution.py:235
  50.0 0.8 %finish.1 = f32[2,4096]{1,0:T(2,128)} custom-call(f32[80,128]{1,0:T(8,128)S(1)} %collective-permute-done.9.moved_ref, f32[16,128]{1,0:T(8,128)S(1)} %bitcast.8), custom_call_target="tpu_custom_call" | custom-call | tf_op jit(solution)/shard_map/finish/pallas_call | solution.py:236
  (2 shorter events, 0.0 us)
Async XLA Ops:
  0.0 7.2 %copy-start = (f32[1,2,4096]{2,1,0:T(2,128)S(1)}, f32[1,2,4096]{2,1,0:T(2,128)}, u32[]{:S(2)}) copy-start(f32[1,2,4096]{2,1,0:T(2,128)} %param.10) | copy-start | bytes 98308
  4.9 5.4 %collective-permute-start = (f32[264,128]{1,0:T(8,128)S(1)}, f32[264,128]{1,0:T(8,128)S(1)}, u32[]{:S(2)}, u32[]{:S(2)}) collective-permute-start(f32[264,128]{1,0:T(8,128)S(1)} %products.1.all_refs_0_), channel_id=1, source_target_pairs={{0,16},{16,0},{1,17},{17,1},{2,18},{18,2},{3,19},{19,3},{4,20},{20... | collective-permute-start | bytes 405512 | tf_op jit(solution)/shard_map/ppermute | solution.py:208
  7.3 1.3 %collective-permute-start.1 = (f32[2,64,64]{2,1,0:T(8,128)S(1)}, f32[2,64,64]{2,1,0:T(8,128)S(1)}, u32[]{:S(2)}, u32[]{:S(2)}) collective-permute-start(f32[2,64,64]{2,1,0:T(8,128)S(1)} %reshape.13.projector_ref), channel_id=1, source_target_pairs={{0,1},{1,0},{2,3},{3,2},{4,5},{5,4},{6,7},{7,6},{8,9},{9,8},{10,11... | collective-permute-start | bytes 98312 | tf_op jit(solution)/shard_map/ppermute | solution.py:211
  7.4 2.9 %collective-permute-start.3 = (f32[264,128]{1,0:T(8,128)S(1)}, f32[264,128]{1,0:T(8,128)S(1)}, u32[]{:S(2)}, u32[]{:S(2)}) collective-permute-start(f32[264,128]{1,0:T(8,128)S(1)} %products.1.all_refs_0_), channel_id=1, source_target_pairs={{0,1},{1,0},{2,3},{3,2},{4,5},{5,4},{6,7},{7,6},{8,9},{9,8},{10,11... | collective-permute-start | bytes 405512 | tf_op jit(solution)/shard_map/ppermute | solution.py:209
  10.3 1.4 %collective-permute-start.2 = (f32[264,128]{1,0:T(8,128)S(1)}, f32[264,128]{1,0:T(8,128)S(1)}, u32[]{:S(2)}, u32[]{:S(2)}) collective-permute-start(f32[264,128]{1,0:T(8,128)S(1)} %collective-permute-done.all_refs_0_), channel_id=1, source_target_pairs={{0,1},{1,0},{2,3},{3,2},{4,5},{5,4},{6,7},{7,6},{8,9},{9,8},{10,11... | collective-permute-start | bytes 405512 | tf_op jit(solution)/shard_map/ppermute | solution.py:213
  11.9 9.9 %collective-permute-start.4 = (f32[2,64,128]{2,1,0:T(8,128)S(1)}, f32[2,64,128]{2,1,0:T(8,128)S(1)}, u32[]{:S(2)}, u32[]{:S(2)}) collective-permute-start(f32[2,64,128]{2,1,0:T(8,128)S(1)} %get-tuple-element.34), channel_id=1, source_target_pairs={{0,8},{1,11},{2,10},{3,13},{4,12},{5,15},{6,14},{7,1},{8,0},{9,3},... | collective-permute-start | bytes 196616 | tf_op jit(solution)/shard_map/ppermute | solution.py:221
  19.2 8.4 %collective-permute-start.5 = (f32[2,64,128]{2,1,0:T(8,128)S(1)}, f32[2,64,128]{2,1,0:T(8,128)S(1)}, u32[]{:S(2)}, u32[]{:S(2)}) collective-permute-start(f32[2,64,128]{2,1,0:T(8,128)S(1)} %get-tuple-element.35), channel_id=1, source_target_pairs={{0,6},{1,13},{2,8},{3,15},{4,10},{5,1},{6,12},{7,3},{8,14},{9,5},{... | collective-permute-start | bytes 196616 | tf_op jit(solution)/shard_map/ppermute | solution.py:221
  21.1 6.7 %collective-permute-start.6 = (f32[2,64,128]{2,1,0:T(8,128)S(1)}, f32[2,64,128]{2,1,0:T(8,128)S(1)}, u32[]{:S(2)}, u32[]{:S(2)}) collective-permute-start(f32[2,64,128]{2,1,0:T(8,128)S(1)} %get-tuple-element.36), channel_id=1, source_target_pairs={{0,2},{1,5},{2,4},{3,7},{4,6},{5,9},{6,8},{7,11},{8,10},{9,13},{10... | collective-permute-start | bytes 196616 | tf_op jit(solution)/shard_map/ppermute | solution.py:221
  21.1 6.7 %collective-permute-start.7 = (f32[2,64,128]{2,1,0:T(8,128)S(1)}, f32[2,64,128]{2,1,0:T(8,128)S(1)}, u32[]{:S(2)}, u32[]{:S(2)}) collective-permute-start(f32[2,64,128]{2,1,0:T(8,128)S(1)} %get-tuple-element.37), channel_id=1, source_target_pairs={{1,15},{3,1},{5,3},{7,5},{9,7},{11,9},{13,11},{15,13},{17,31},{19,... | collective-permute-start | bytes 196616 | tf_op jit(solution)/shard_map/ppermute | solution.py:221
  27.8 1.3 %collective-permute-start.8 = (f32[2,64,128]{2,1,0:T(8,128)S(1)}, f32[2,64,128]{2,1,0:T(8,128)S(1)}, u32[]{:S(2)}, u32[]{:S(2)}) collective-permute-start(f32[2,64,128]{2,1,0:T(8,128)S(1)} %gather.1.mine_ref), channel_id=1, source_target_pairs={{0,1},{1,0},{2,3},{3,2},{4,5},{5,4},{6,7},{7,6},{8,9},{9,8},{10,11... | collective-permute-start | bytes 196616 | tf_op jit(solution)/shard_map/ppermute | solution.py:225
  29.8 7.7 %collective-permute-start.9 = (f32[80,128]{1,0:T(8,128)S(1)}, f32[80,128]{1,0:T(8,128)S(1)}, u32[]{:S(2)}, u32[]{:S(2)}) collective-permute-start(f32[80,128]{1,0:T(8,128)S(1)} %project.1), channel_id=1, source_target_pairs={{0,32},{32,64},{64,96},{96,128},{128,160},{160,192},{192,224},{224... | collective-permute-start | bytes 122888 | tf_op jit(solution)/shard_map/ppermute | solution.py:234

commit v6 on v5

--- a/solution.py
+++ b/solution.py
@@ -87,7 +87,8 @@
         msg_ref[pl.ds(t * B, B), :] = jnp.where(low, total[:B], total[B:])
 
 
-HOPS = ((4, -3), (3, -2), (1, 2), (0, -1))
+LEAD = [8 * x + z for z in range(ZS - 1, -1, -1) for x in range(2)]
+HOPS = ((4, -3), (3, -2), (-1, 2), (0, 1))
 
 
 def place_kernel(count, before, *all_refs):
@@ -232,7 +233,7 @@
         name="project",
     )(mine, beside, projector, other)
     moved = lax.ppermute(payload, "col", [(i, (i + 1) % 8) for i in range(8)])
-    tops = lax.all_to_all(moved[B:], ("xl", "z"), 0, 0, tiled=True)
+    tops = lax.all_to_all(moved[B:], ("xl", "z"), 0, 0, tiled=True, axis_index_groups=[LEAD])
     return pl.pallas_call(
         finish_kernel,
         out_shape=jax.ShapeDtypeStruct((2, B * B), F32),

time: 51 us -> 49.3 us (0.967)
  starting transfers between devices: 15 us -> 17.3 us
  blocking collectives: 12.6 us -> 10.4 us
  waiting for transfers between devices: 15.8 us -> 13.9 us
    ppermute x4, starting transfers between devices: 9.85 us -> 12.1 us  [along(): return lax.ppermute(x, ('z', 'core'), moves)]
    all_to_all x1, blocking collectives: 12.6 us -> 10.4 us  [local(): lax.all_to_all(moved[B:], ('xl', 'z'), 0, 0, tiled=True, axis_index_group...]
    ppermute x4, waiting for transfers between devices: 6.01 us -> 4.2 us  [along(): return lax.ppermute(x, ('z', 'core'), moves)]
  transfers between devices with their start and end apart: 10 -> 10, of which waited for: 7 -> 6; matrix products, arithmetic and copies ran while one was open for 0% -> 0% of each run, Pallas kernels for 1% -> 1%
where the time goes in v6:
time: 49.3 us; the launch traced here: 49.1 us
  starting transfers between devices  17.3 us (35%)
  waiting for transfers between devices  13.9 us (28%)
  blocking collectives  10.4 us (21%)
  Pallas kernels  7.33 us (15%)
    ppermute x4, starting transfers between devices, along(): return lax.ppermute(x, ('z', 'core'), moves)  12.1 us
    all_to_all x1, blocking collectives, local(): lax.all_to_all(moved[B:], ('xl', 'z'), 0, 0, tiled=True, axis_index_group...  10.4 us
    ppermute x1, waiting for transfers between devices, local(): moved = lax.ppermute(payload, 'col', [(i, (i + 1) % 8) for i in range(8)])  5.48 us
    pallas_call x1, Pallas kernels, local(): pl.pallas_call(products_kernel, out_shape=pltpu.VMEM((MSG + PAIRS, 2 * B)...  4.87 us
    ppermute x4, waiting for transfers between devices, along(): return lax.ppermute(x, ('z', 'core'), moves)  4.2 us
    ppermute x1, starting transfers between devices, local(): over = lax.ppermute(message, 'xl', SWAP)  2.36 us
    ppermute x1, starting transfers between devices, local(): moved = lax.ppermute(payload, 'col', [(i, (i + 1) % 8) for i in range(8)])  2.21 us
    ppermute x1, waiting for transfers between devices, local(): over = lax.ppermute(message, 'xl', SWAP)  1.66 us
  transfers between devices with their start and end apart: 10, of which 6 were waited for; matrix products, arithmetic and copies ran while one was open for 0% of the time, Pallas kernels for 1%

profile of v6, /device:TPU:2, one launch (start us, length us, event | category | flops | bytes accessed | tf_op | source)
XLA Modules:
  0.0 49.1 jit_solution(18037044787214531903)
XLA Ops:
  0.0 0.0 copy-start
  0.0 4.9 %products.1.all_refs_0_ = f32[264,128]{1,0:T(8,128)S(1)} custom-call(s32[1,8]{1,0:T(1,128)} %left_hbm.1, s32[1,8]{1,0:T(1,128)} %out_hbm.1, s32[64]{0:T(128)} %owner_hbm.1, bf16[2,4096]{1,0:T(2,128)(2,1)} %bitcast.12, bf16[512,4096]{1,0:T(8,128)(2,1)} %bitcast.9, bf16[512,4096]{1,0:T(8,128)(2,1)} %bitcast.10), custom_call_target="tpu_custom_call" | custom-call | tf_op jit(solution)/shard_map/products/pallas_call | solution.py:187
  4.9 2.4 %collective-permute-start = (f32[264,128]{1,0:T(8,128)S(1)}, f32[264,128]{1,0:T(8,128)S(1)}, u32[]{:S(2)}, u32[]{:S(2)}) collective-permute-start(f32[264,128]{1,0:T(8,128)S(1)} %products.1.all_refs_0_), channel_id=1, source_target_pairs={{0,16},{16,0},{1,17},{17,1},{2,18},{18,2},{3,19},{19,3},{4,20},{20... | collective-permute-start | bytes 405512 | tf_op jit(solution)/shard_map/ppermute | solution.py:209
  7.2 0.0 copy-done
  7.2 0.1 reshape.13.projector_ref
  7.3 0.0 collective-permute-start.1
  7.4 0.5 %collective-permute-start.3 = (f32[264,128]{1,0:T(8,128)S(1)}, f32[264,128]{1,0:T(8,128)S(1)}, u32[]{:S(2)}, u32[]{:S(2)}) collective-permute-start(f32[264,128]{1,0:T(8,128)S(1)} %products.1.all_refs_0_), channel_id=1, source_target_pairs={{0,1},{1,0},{2,3},{3,2},{4,5},{5,4},{6,7},{7,6},{8,9},{9,8},{10,11... | collective-permute-start | bytes 405512 | tf_op jit(solution)/shard_map/ppermute | solution.py:210
  7.9 0.7 %collective-permute-done.1.other_ref = f32[2,64,64]{2,1,0:T(8,128)S(1)} collective-permute-done((f32[2,64,64]{2,1,0:T(8,128)S(1)}, f32[2,64,64]{2,1,0:T(8,128)S(1)}, u32[]{:S(2)}, u32[]{:S(2)}) %collective-permute-start.1) | collective-permute-done | bytes 32800 | tf_op jit(solution)/shard_map/ppermute | solution.py:212
  8.6 1.7 %collective-permute-done.all_refs_0_ = f32[264,128]{1,0:T(8,128)S(1)} collective-permute-done((f32[264,128]{1,0:T(8,128)S(1)}, f32[264,128]{1,0:T(8,128)S(1)}, u32[]{:S(2)}, u32[]{:S(2)}) %collective-permute-start) | collective-permute-done | bytes 135200 | tf_op jit(solution)/shard_map/ppermute | solution.py:209
  10.3 0.0 collective-permute-start.2
  10.3 0.0 collective-permute-done.3.all_refs_1_
  10.3 0.5 place.3
  10.8 0.3 place.4
  11.0 0.6 %collective-permute-done.2.all_refs_0_ = f32[264,128]{1,0:T(8,128)S(1)} collective-permute-done((f32[264,128]{1,0:T(8,128)S(1)}, f32[264,128]{1,0:T(8,128)S(1)}, u32[]{:S(2)}, u32[]{:S(2)}) %collective-permute-start.2) | collective-permute-done | bytes 135200 | tf_op jit(solution)/shard_map/ppermute | solution.py:214
  11.6 0.2 place.5
  11.9 7.3 %collective-permute-start.4 = (f32[2,64,128]{2,1,0:T(8,128)S(1)}, f32[2,64,128]{2,1,0:T(8,128)S(1)}, u32[]{:S(2)}, u32[]{:S(2)}) collective-permute-start(f32[2,64,128]{2,1,0:T(8,128)S(1)} %get-tuple-element.34), channel_id=1, source_target_pairs={{0,8},{1,11},{2,10},{3,13},{4,12},{5,15},{6,14},{7,1},{8,0},{9,3},... | collective-permute-start | bytes 196616 | tf_op jit(solution)/shard_map/ppermute | solution.py:222
  19.2 1.9 %collective-permute-start.5 = (f32[2,64,128]{2,1,0:T(8,128)S(1)}, f32[2,64,128]{2,1,0:T(8,128)S(1)}, u32[]{:S(2)}, u32[]{:S(2)}) collective-permute-start(f32[2,64,128]{2,1,0:T(8,128)S(1)} %get-tuple-element.35), channel_id=1, source_target_pairs={{0,6},{1,13},{2,8},{3,15},{4,10},{5,1},{6,12},{7,3},{8,14},{9,5},{... | collective-permute-start | bytes 196616 | tf_op jit(solution)/shard_map/ppermute | solution.py:222
  21.1 2.2 %collective-permute-start.6 = (f32[2,64,128]{2,1,0:T(8,128)S(1)}, f32[2,64,128]{2,1,0:T(8,128)S(1)}, u32[]{:S(2)}, u32[]{:S(2)}) collective-permute-start(f32[2,64,128]{2,1,0:T(8,128)S(1)} %get-tuple-element.36), channel_id=1, source_target_pairs={{0,14},{1,5},{2,0},{3,7},{4,2},{5,9},{6,4},{7,11},{8,6},{9,13},{10... | collective-permute-start | bytes 196616 | tf_op jit(solution)/shard_map/ppermute | solution.py:222
  23.3 0.7 %collective-permute-start.7 = (f32[2,64,128]{2,1,0:T(8,128)S(1)}, f32[2,64,128]{2,1,0:T(8,128)S(1)}, u32[]{:S(2)}, u32[]{:S(2)}) collective-permute-start(f32[2,64,128]{2,1,0:T(8,128)S(1)} %get-tuple-element.37), channel_id=1, source_target_pairs={{1,3},{3,5},{5,7},{7,9},{9,11},{11,13},{13,15},{15,1},{17,19},{19,... | collective-permute-start | bytes 196616 | tf_op jit(solution)/shard_map/ppermute | solution.py:222
  24.0 0.0 collective-permute-done.4.refs_0_
  24.0 4.2 %collective-permute-done.5.refs_1_ = f32[2,64,128]{2,1,0:T(8,128)S(1)} collective-permute-done((f32[2,64,128]{2,1,0:T(8,128)S(1)}, f32[2,64,128]{2,1,0:T(8,128)S(1)}, u32[]{:S(2)}, u32[]{:S(2)}) %collective-permute-start.5) | collective-permute-done | bytes 65568 | tf_op jit(solution)/shard_map/ppermute | solution.py:222
  28.2 0.0 collective-permute-done.6.refs_2_
  28.2 0.0 collective-permute-done.7.refs_3_
  28.2 0.1 collective-permute-start.8
  28.3 1.2 %collective-permute-done.8.beside_ref = f32[2,64,128]{2,1,0:T(8,128)S(1)} collective-permute-done((f32[2,64,128]{2,1,0:T(8,128)S(1)}, f32[2,64,128]{2,1,0:T(8,128)S(1)}, u32[]{:S(2)}, u32[]{:S(2)}) %collective-permute-start.8) | collective-permute-done | bytes 65568 | tf_op jit(solution)/shard_map/ppermute | solution.py:226
  29.6 0.6 %project.1 = f32[80,128]{1,0:T(8,128)S(1)} custom-call(f32[2,64,128]{2,1,0:T(8,128)S(1)} %gather.1.mine_ref, f32[2,64,128]{2,1,0:T(8,128)S(1)} %collective-permute-done.8.beside_ref, f32[2,64,64]{2,1,0:T(8,128)S(1)} %reshape.13.projector_ref, f32[2,64,64]{2,1,0:T(8,128)S(1)} %collective-permute-done.1.other_ref), custom_call_target="tpu_custom_call" | custom-call | tf_op jit(solution)/shard_map/project/pallas_call | solution.py:227
  30.2 2.2 %collective-permute-start.9 = (f32[80,128]{1,0:T(8,128)S(1)}, f32[80,128]{1,0:T(8,128)S(1)}, u32[]{:S(2)}, u32[]{:S(2)}) collective-permute-start(f32[80,128]{1,0:T(8,128)S(1)} %project.1), channel_id=1, source_target_pairs={{0,32},{32,64},{64,96},{96,128},{128,160},{160,192},{192,224},{224... | collective-permute-start | bytes 122888 | tf_op jit(solution)/shard_map/ppermute | solution.py:235
  32.4 5.5 %collective-permute-done.9.moved_ref = f32[80,128]{1,0:T(8,128)S(1)} collective-permute-done((f32[80,128]{1,0:T(8,128)S(1)}, f32[80,128]{1,0:T(8,128)S(1)}, u32[]{:S(2)}, u32[]{:S(2)}) %collective-permute-start.9) | collective-permute-done | bytes 40992 | tf_op jit(solution)/shard_map/ppermute | solution.py:235
  37.9 10.4 %all_to_all.11 = f32[16,1,128]{2,1,0:T(1,128)S(1)} all-to-all(f32[16,1,128]{2,1,0:T(1,128)S(1)} %bitcast.11), channel_id=1, replica_groups={{14,30,12,28,10,26,8,24,6,22,4,20,2,18,0,16},{15,31,13,29,11,27,9,25,7,..., dimensions={0} | all-to-all | bytes 16384 | tf_op jit(solution)/shard_map/all_to_all | solution.py:236
  48.3 0.8 %finish.1 = f32[2,4096]{1,0:T(2,128)} custom-call(f32[80,128]{1,0:T(8,128)S(1)} %collective-permute-done.9.moved_ref, f32[16,128]{1,0:T(8,128)S(1)} %bitcast.8), custom_call_target="tpu_custom_call" | custom-call | tf_op jit(solution)/shard_map/finish/pallas_call | solution.py:237
  (2 shorter events, 0.0 us)
Async XLA Ops:
  0.0 7.2 %copy-start = (f32[1,2,4096]{2,1,0:T(2,128)S(1)}, f32[1,2,4096]{2,1,0:T(2,128)}, u32[]{:S(2)}) copy-start(f32[1,2,4096]{2,1,0:T(2,128)} %param.10) | copy-start | bytes 98308
  4.9 5.4 %collective-permute-start = (f32[264,128]{1,0:T(8,128)S(1)}, f32[264,128]{1,0:T(8,128)S(1)}, u32[]{:S(2)}, u32[]{:S(2)}) collective-permute-start(f32[264,128]{1,0:T(8,128)S(1)} %products.1.all_refs_0_), channel_id=1, source_target_pairs={{0,16},{16,0},{1,17},{17,1},{2,18},{18,2},{3,19},{19,3},{4,20},{20... | collective-permute-start | bytes 405512 | tf_op jit(solution)/shard_map/ppermute | solution.py:209
  7.3 1.3 %collective-permute-start.1 = (f32[2,64,64]{2,1,0:T(8,128)S(1)}, f32[2,64,64]{2,1,0:T(8,128)S(1)}, u32[]{:S(2)}, u32[]{:S(2)}) collective-permute-start(f32[2,64,64]{2,1,0:T(8,128)S(1)} %reshape.13.projector_ref), channel_id=1, source_target_pairs={{0,1},{1,0},{2,3},{3,2},{4,5},{5,4},{6,7},{7,6},{8,9},{9,8},{10,11... | collective-permute-start | bytes 98312 | tf_op jit(solution)/shard_map/ppermute | solution.py:212
  7.4 2.9 %collective-permute-start.3 = (f32[264,128]{1,0:T(8,128)S(1)}, f32[264,128]{1,0:T(8,128)S(1)}, u32[]{:S(2)}, u32[]{:S(2)}) collective-permute-start(f32[264,128]{1,0:T(8,128)S(1)} %products.1.all_refs_0_), channel_id=1, source_target_pairs={{0,1},{1,0},{2,3},{3,2},{4,5},{5,4},{6,7},{7,6},{8,9},{9,8},{10,11... | collective-permute-start | bytes 405512 | tf_op jit(solution)/shard_map/ppermute | solution.py:210
  10.3 1.4 %collective-permute-start.2 = (f32[264,128]{1,0:T(8,128)S(1)}, f32[264,128]{1,0:T(8,128)S(1)}, u32[]{:S(2)}, u32[]{:S(2)}) collective-permute-start(f32[264,128]{1,0:T(8,128)S(1)} %collective-permute-done.all_refs_0_), channel_id=1, source_target_pairs={{0,1},{1,0},{2,3},{3,2},{4,5},{5,4},{6,7},{7,6},{8,9},{9,8},{10,11... | collective-permute-start | bytes 405512 | tf_op jit(solution)/shard_map/ppermute | solution.py:214
  11.9 12.1 %collective-permute-start.4 = (f32[2,64,128]{2,1,0:T(8,128)S(1)}, f32[2,64,128]{2,1,0:T(8,128)S(1)}, u32[]{:S(2)}, u32[]{:S(2)}) collective-permute-start(f32[2,64,128]{2,1,0:T(8,128)S(1)} %get-tuple-element.34), channel_id=1, source_target_pairs={{0,8},{1,11},{2,10},{3,13},{4,12},{5,15},{6,14},{7,1},{8,0},{9,3},... | collective-permute-start | bytes 196616 | tf_op jit(solution)/shard_map/ppermute | solution.py:222
  19.2 9.0 %collective-permute-start.5 = (f32[2,64,128]{2,1,0:T(8,128)S(1)}, f32[2,64,128]{2,1,0:T(8,128)S(1)}, u32[]{:S(2)}, u32[]{:S(2)}) collective-permute-start(f32[2,64,128]{2,1,0:T(8,128)S(1)} %get-tuple-element.35), channel_id=1, source_target_pairs={{0,6},{1,13},{2,8},{3,15},{4,10},{5,1},{6,12},{7,3},{8,14},{9,5},{... | collective-permute-start | bytes 196616 | tf_op jit(solution)/shard_map/ppermute | solution.py:222
  21.1 7.1 %collective-permute-start.6 = (f32[2,64,128]{2,1,0:T(8,128)S(1)}, f32[2,64,128]{2,1,0:T(8,128)S(1)}, u32[]{:S(2)}, u32[]{:S(2)}) collective-permute-start(f32[2,64,128]{2,1,0:T(8,128)S(1)} %get-tuple-element.36), channel_id=1, source_target_pairs={{0,14},{1,5},{2,0},{3,7},{4,2},{5,9},{6,4},{7,11},{8,6},{9,13},{10... | collective-permute-start | bytes 196616 | tf_op jit(solution)/shard_map/ppermute | solution.py:222
  23.3 4.9 %collective-permute-start.7 = (f32[2,64,128]{2,1,0:T(8,128)S(1)}, f32[2,64,128]{2,1,0:T(8,128)S(1)}, u32[]{:S(2)}, u32[]{:S(2)}) collective-permute-start(f32[2,64,128]{2,1,0:T(8,128)S(1)} %get-tuple-element.37), channel_id=1, source_target_pairs={{1,3},{3,5},{5,7},{7,9},{9,11},{11,13},{13,15},{15,1},{17,19},{19,... | collective-permute-start | bytes 196616 | tf_op jit(solution)/shard_map/ppermute | solution.py:222
  28.2 1.3 %collective-permute-start.8 = (f32[2,64,128]{2,1,0:T(8,128)S(1)}, f32[2,64,128]{2,1,0:T(8,128)S(1)}, u32[]{:S(2)}, u32[]{:S(2)}) collective-permute-start(f32[2,64,128]{2,1,0:T(8,128)S(1)} %gather.1.mine_ref), channel_id=1, source_target_pairs={{0,1},{1,0},{2,3},{3,2},{4,5},{5,4},{6,7},{7,6},{8,9},{9,8},{10,11... | collective-permute-start | bytes 196616 | tf_op jit(solution)/shard_map/ppermute | solution.py:226
  30.2 7.7 %collective-permute-start.9 = (f32[80,128]{1,0:T(8,128)S(1)}, f32[80,128]{1,0:T(8,128)S(1)}, u32[]{:S(2)}, u32[]{:S(2)}) collective-permute-start(f32[80,128]{1,0:T(8,128)S(1)} %project.1), channel_id=1, source_target_pairs={{0,32},{32,64},{64,96},{96,128},{128,160},{160,192},{192,224},{224... | collective-permute-start | bytes 122888 | tf_op jit(solution)/shard_map/ppermute | solution.py:235

commit v7 on v6

--- a/solution.py
+++ b/solution.py
@@ -87,8 +87,8 @@
         msg_ref[pl.ds(t * B, B), :] = jnp.where(low, total[:B], total[B:])
 
 
-LEAD = [8 * x + z for z in range(ZS - 1, -1, -1) for x in range(2)]
-HOPS = ((4, -3), (3, -2), (-1, 2), (0, 1))
+LEAD = [8 * x + z for z in (5, 4, 3, 2, 1, 0, 7, 6) for x in range(2)]
+HOPS = ((4, -3), (-2, 3), (-1, 2), (0, 1))
 
 
 def place_kernel(count, before, *all_refs):

time: 49.3 us -> 48.1 us (0.976)
  starting transfers between devices: 17.3 us -> 15.2 us
  waiting for transfers between devices: 13.9 us -> 14.8 us
    ppermute x4, starting transfers between devices: 12.1 us -> 8.13 us  [along(): return lax.ppermute(x, ('z', 'core'), moves)]
    ppermute x1, starting transfers between devices: 0.09 us -> 2 us  [local(): beside = lax.ppermute(mine, 'core', SWAP)]
    ppermute x4, waiting for transfers between devices: 4.2 us -> 5.38 us  [along(): return lax.ppermute(x, ('z', 'core'), moves)]
  transfers between devices with their start and end apart: 10 -> 10, of which waited for: 6 -> 8; matrix products, arithmetic and copies ran while one was open for 0% -> 0% of each run, Pallas kernels for 1% -> 2%
where the time goes in v7:
time: 48.1 us; the launch traced here: 48 us
  starting transfers between devices  15.2 us (32%)
  waiting for transfers between devices  14.8 us (31%)
  blocking collectives  10.5 us (22%)
  Pallas kernels  7.33 us (15%)
    all_to_all x1, blocking collectives, local(): lax.all_to_all(moved[B:], ('xl', 'z'), 0, 0, tiled=True, axis_index_group...  10.5 us
    ppermute x4, starting transfers between devices, along(): return lax.ppermute(x, ('z', 'core'), moves)  8.13 us
    ppermute x1, waiting for transfers between devices, local(): moved = lax.ppermute(payload, 'col', [(i, (i + 1) % 8) for i in range(8)])  5.49 us
    ppermute x4, waiting for transfers between devices, along(): return lax.ppermute(x, ('z', 'core'), moves)  5.38 us
    pallas_call x1, Pallas kernels, local(): pl.pallas_call(products_kernel, out_shape=pltpu.VMEM((MSG + PAIRS, 2 * B)...  4.87 us
    ppermute x1, starting transfers between devices, local(): over = lax.ppermute(message, 'xl', SWAP)  2.36 us
    ppermute x1, starting transfers between devices, local(): moved = lax.ppermute(payload, 'col', [(i, (i + 1) % 8) for i in range(8)])  2.2 us
    ppermute x1, starting transfers between devices, local(): beside = lax.ppermute(mine, 'core', SWAP)  2 us
  transfers between devices with their start and end apart: 10, of which 8 were waited for; matrix products, arithmetic and copies ran while one was open for 0% of the time, Pallas kernels for 2%

profile of v7, /device:TPU:2, one launch (start us, length us, event | category | flops | bytes accessed | tf_op | source)
XLA Modules:
  0.0 48.0 jit_solution(16032566520691946398)
XLA Ops:
  0.0 0.0 copy-start
  0.0 4.9 %products.1.all_refs_0_ = f32[264,128]{1,0:T(8,128)S(1)} custom-call(s32[1,8]{1,0:T(1,128)} %left_hbm.1, s32[1,8]{1,0:T(1,128)} %out_hbm.1, s32[64]{0:T(128)} %owner_hbm.1, bf16[2,4096]{1,0:T(2,128)(2,1)} %bitcast.12, bf16[512,4096]{1,0:T(8,128)(2,1)} %bitcast.9, bf16[512,4096]{1,0:T(8,128)(2,1)} %bitcast.10), custom_call_target="tpu_custom_call" | custom-call | tf_op jit(solution)/shard_map/products/pallas_call | solution.py:187
  4.9 2.4 %collective-permute-start = (f32[264,128]{1,0:T(8,128)S(1)}, f32[264,128]{1,0:T(8,128)S(1)}, u32[]{:S(2)}, u32[]{:S(2)}) collective-permute-start(f32[264,128]{1,0:T(8,128)S(1)} %products.1.all_refs_0_), channel_id=1, source_target_pairs={{0,16},{16,0},{1,17},{17,1},{2,18},{18,2},{3,19},{19,3},{4,20},{20... | collective-permute-start | bytes 405512 | tf_op jit(solution)/shard_map/ppermute | solution.py:209
  7.2 0.0 copy-done
  7.2 0.1 reshape.13.projector_ref
  7.3 0.0 collective-permute-start.1
  7.4 0.5 %collective-permute-start.3 = (f32[264,128]{1,0:T(8,128)S(1)}, f32[264,128]{1,0:T(8,128)S(1)}, u32[]{:S(2)}, u32[]{:S(2)}) collective-permute-start(f32[264,128]{1,0:T(8,128)S(1)} %products.1.all_refs_0_), channel_id=1, source_target_pairs={{0,1},{1,0},{2,3},{3,2},{4,5},{5,4},{6,7},{7,6},{8,9},{9,8},{10,11... | collective-permute-start | bytes 405512 | tf_op jit(solution)/shard_map/ppermute | solution.py:210
  7.9 0.7 %collective-permute-done.1.other_ref = f32[2,64,64]{2,1,0:T(8,128)S(1)} collective-permute-done((f32[2,64,64]{2,1,0:T(8,128)S(1)}, f32[2,64,64]{2,1,0:T(8,128)S(1)}, u32[]{:S(2)}, u32[]{:S(2)}) %collective-permute-start.1) | collective-permute-done | bytes 32800 | tf_op jit(solution)/shard_map/ppermute | solution.py:212
  8.6 1.7 %collective-permute-done.all_refs_0_ = f32[264,128]{1,0:T(8,128)S(1)} collective-permute-done((f32[264,128]{1,0:T(8,128)S(1)}, f32[264,128]{1,0:T(8,128)S(1)}, u32[]{:S(2)}, u32[]{:S(2)}) %collective-permute-start) | collective-permute-done | bytes 135200 | tf_op jit(solution)/shard_map/ppermute | solution.py:209
  10.3 0.0 collective-permute-start.2
  10.3 0.0 collective-permute-done.3.all_refs_1_
  10.3 0.5 place.3
  10.8 0.3 place.4
  11.0 0.6 %collective-permute-done.2.all_refs_0_ = f32[264,128]{1,0:T(8,128)S(1)} collective-permute-done((f32[264,128]{1,0:T(8,128)S(1)}, f32[264,128]{1,0:T(8,128)S(1)}, u32[]{:S(2)}, u32[]{:S(2)}) %collective-permute-start.2) | collective-permute-done | bytes 135200 | tf_op jit(solution)/shard_map/ppermute | solution.py:214
  11.6 0.2 place.5
  11.9 7.3 %collective-permute-start.4 = (f32[2,64,128]{2,1,0:T(8,128)S(1)}, f32[2,64,128]{2,1,0:T(8,128)S(1)}, u32[]{:S(2)}, u32[]{:S(2)}) collective-permute-start(f32[2,64,128]{2,1,0:T(8,128)S(1)} %get-tuple-element.34), channel_id=1, source_target_pairs={{0,8},{1,11},{2,10},{3,13},{4,12},{5,15},{6,14},{7,1},{8,0},{9,3},... | collective-permute-start | bytes 196616 | tf_op jit(solution)/shard_map/ppermute | solution.py:222
  19.2 0.0 collective-permute-start.5
  19.2 0.2 collective-permute-start.6
  19.4 0.7 %collective-permute-start.7 = (f32[2,64,128]{2,1,0:T(8,128)S(1)}, f32[2,64,128]{2,1,0:T(8,128)S(1)}, u32[]{:S(2)}, u32[]{:S(2)}) collective-permute-start(f32[2,64,128]{2,1,0:T(8,128)S(1)} %get-tuple-element.37), channel_id=1, source_target_pairs={{1,3},{3,5},{5,7},{7,9},{9,11},{11,13},{13,15},{15,1},{17,19},{19,... | collective-permute-start | bytes 196616 | tf_op jit(solution)/shard_map/ppermute | solution.py:222
  20.0 1.9 %collective-permute-done.4.refs_0_ = f32[2,64,128]{2,1,0:T(8,128)S(1)} collective-permute-done((f32[2,64,128]{2,1,0:T(8,128)S(1)}, f32[2,64,128]{2,1,0:T(8,128)S(1)}, u32[]{:S(2)}, u32[]{:S(2)}) %collective-permute-start.4) | collective-permute-done | bytes 65568 | tf_op jit(solution)/shard_map/ppermute | solution.py:222
  21.9 3.3 %collective-permute-done.5.refs_1_ = f32[2,64,128]{2,1,0:T(8,128)S(1)} collective-permute-done((f32[2,64,128]{2,1,0:T(8,128)S(1)}, f32[2,64,128]{2,1,0:T(8,128)S(1)}, u32[]{:S(2)}, u32[]{:S(2)}) %collective-permute-start.5) | collective-permute-done | bytes 65568 | tf_op jit(solution)/shard_map/ppermute | solution.py:222
  25.2 0.2 collective-permute-done.6.refs_2_
  25.4 0.0 collective-permute-done.7.refs_3_
  25.4 2.0 %collective-permute-start.8 = (f32[2,64,128]{2,1,0:T(8,128)S(1)}, f32[2,64,128]{2,1,0:T(8,128)S(1)}, u32[]{:S(2)}, u32[]{:S(2)}) collective-permute-start(f32[2,64,128]{2,1,0:T(8,128)S(1)} %gather.1.mine_ref), channel_id=1, source_target_pairs={{0,1},{1,0},{2,3},{3,2},{4,5},{5,4},{6,7},{7,6},{8,9},{9,8},{10,11... | collective-permute-start | bytes 196616 | tf_op jit(solution)/shard_map/ppermute | solution.py:226
  27.4 0.9 %collective-permute-done.8.beside_ref = f32[2,64,128]{2,1,0:T(8,128)S(1)} collective-permute-done((f32[2,64,128]{2,1,0:T(8,128)S(1)}, f32[2,64,128]{2,1,0:T(8,128)S(1)}, u32[]{:S(2)}, u32[]{:S(2)}) %collective-permute-start.8) | collective-permute-done | bytes 65568 | tf_op jit(solution)/shard_map/ppermute | solution.py:226
  28.3 0.6 %project.1 = f32[80,128]{1,0:T(8,128)S(1)} custom-call(f32[2,64,128]{2,1,0:T(8,128)S(1)} %gather.1.mine_ref, f32[2,64,128]{2,1,0:T(8,128)S(1)} %collective-permute-done.8.beside_ref, f32[2,64,64]{2,1,0:T(8,128)S(1)} %reshape.13.projector_ref, f32[2,64,64]{2,1,0:T(8,128)S(1)} %collective-permute-done.1.other_ref), custom_call_target="tpu_custom_call" | custom-call | tf_op jit(solution)/shard_map/project/pallas_call | solution.py:227
  29.0 2.2 %collective-permute-start.9 = (f32[80,128]{1,0:T(8,128)S(1)}, f32[80,128]{1,0:T(8,128)S(1)}, u32[]{:S(2)}, u32[]{:S(2)}) collective-permute-start(f32[80,128]{1,0:T(8,128)S(1)} %project.1), channel_id=1, source_target_pairs={{0,32},{32,64},{64,96},{96,128},{128,160},{160,192},{192,224},{224... | collective-permute-start | bytes 122888 | tf_op jit(solution)/shard_map/ppermute | solution.py:235
  31.2 5.5 %collective-permute-done.9.moved_ref = f32[80,128]{1,0:T(8,128)S(1)} collective-permute-done((f32[80,128]{1,0:T(8,128)S(1)}, f32[80,128]{1,0:T(8,128)S(1)}, u32[]{:S(2)}, u32[]{:S(2)}) %collective-permute-start.9) | collective-permute-done | bytes 40992 | tf_op jit(solution)/shard_map/ppermute | solution.py:235
  36.7 10.5 %all_to_all.11 = f32[16,1,128]{2,1,0:T(1,128)S(1)} all-to-all(f32[16,1,128]{2,1,0:T(1,128)S(1)} %bitcast.11), channel_id=1, replica_groups={{10,26,8,24,6,22,4,20,2,18,0,16,14,30,12,28},{11,27,9,25,7,23,5,21,3,19..., dimensions={0} | all-to-all | bytes 16384 | tf_op jit(solution)/shard_map/all_to_all | solution.py:236
  47.1 0.8 %finish.1 = f32[2,4096]{1,0:T(2,128)} custom-call(f32[80,128]{1,0:T(8,128)S(1)} %collective-permute-done.9.moved_ref, f32[16,128]{1,0:T(8,128)S(1)} %bitcast.8), custom_call_target="tpu_custom_call" | custom-call | tf_op jit(solution)/shard_map/finish/pallas_call | solution.py:237
  (2 shorter events, 0.0 us)
Async XLA Ops:
  0.0 7.2 %copy-start = (f32[1,2,4096]{2,1,0:T(2,128)S(1)}, f32[1,2,4096]{2,1,0:T(2,128)}, u32[]{:S(2)}) copy-start(f32[1,2,4096]{2,1,0:T(2,128)} %param.10) | copy-start | bytes 98308
  4.9 5.4 %collective-permute-start = (f32[264,128]{1,0:T(8,128)S(1)}, f32[264,128]{1,0:T(8,128)S(1)}, u32[]{:S(2)}, u32[]{:S(2)}) collective-permute-start(f32[264,128]{1,0:T(8,128)S(1)} %products.1.all_refs_0_), channel_id=1, source_target_pairs={{0,16},{16,0},{1,17},{17,1},{2,18},{18,2},{3,19},{19,3},{4,20},{20... | collective-permute-start | bytes 405512 | tf_op jit(solution)/shard_map/ppermute | solution.py:209
  7.3 1.3 %collective-permute-start.1 = (f32[2,64,64]{2,1,0:T(8,128)S(1)}, f32[2,64,64]{2,1,0:T(8,128)S(1)}, u32[]{:S(2)}, u32[]{:S(2)}) collective-permute-start(f32[2,64,64]{2,1,0:T(8,128)S(1)} %reshape.13.projector_ref), channel_id=1, source_target_pairs={{0,1},{1,0},{2,3},{3,2},{4,5},{5,4},{6,7},{7,6},{8,9},{9,8},{10,11... | collective-permute-start | bytes 98312 | tf_op jit(solution)/shard_map/ppermute | solution.py:212
  7.4 2.9 %collective-permute-start.3 = (f32[264,128]{1,0:T(8,128)S(1)}, f32[264,128]{1,0:T(8,128)S(1)}, u32[]{:S(2)}, u32[]{:S(2)}) collective-permute-start(f32[264,128]{1,0:T(8,128)S(1)} %products.1.all_refs_0_), channel_id=1, source_target_pairs={{0,1},{1,0},{2,3},{3,2},{4,5},{5,4},{6,7},{7,6},{8,9},{9,8},{10,11... | collective-permute-start | bytes 405512 | tf_op jit(solution)/shard_map/ppermute | solution.py:210
  10.3 1.4 %collective-permute-start.2 = (f32[264,128]{1,0:T(8,128)S(1)}, f32[264,128]{1,0:T(8,128)S(1)}, u32[]{:S(2)}, u32[]{:S(2)}) collective-permute-start(f32[264,128]{1,0:T(8,128)S(1)} %collective-permute-done.all_refs_0_), channel_id=1, source_target_pairs={{0,1},{1,0},{2,3},{3,2},{4,5},{5,4},{6,7},{7,6},{8,9},{9,8},{10,11... | collective-permute-start | bytes 405512 | tf_op jit(solution)/shard_map/ppermute | solution.py:214
  11.9 10.0 %collective-permute-start.4 = (f32[2,64,128]{2,1,0:T(8,128)S(1)}, f32[2,64,128]{2,1,0:T(8,128)S(1)}, u32[]{:S(2)}, u32[]{:S(2)}) collective-permute-start(f32[2,64,128]{2,1,0:T(8,128)S(1)} %get-tuple-element.34), channel_id=1, source_target_pairs={{0,8},{1,11},{2,10},{3,13},{4,12},{5,15},{6,14},{7,1},{8,0},{9,3},... | collective-permute-start | bytes 196616 | tf_op jit(solution)/shard_map/ppermute | solution.py:222
  19.2 6.0 %collective-permute-start.5 = (f32[2,64,128]{2,1,0:T(8,128)S(1)}, f32[2,64,128]{2,1,0:T(8,128)S(1)}, u32[]{:S(2)}, u32[]{:S(2)}) collective-permute-start(f32[2,64,128]{2,1,0:T(8,128)S(1)} %get-tuple-element.35), channel_id=1, source_target_pairs={{0,12},{1,7},{2,14},{3,9},{4,0},{5,11},{6,2},{7,13},{8,4},{9,15},{... | collective-permute-start | bytes 196616 | tf_op jit(solution)/shard_map/ppermute | solution.py:222
  19.2 6.2 %collective-permute-start.6 = (f32[2,64,128]{2,1,0:T(8,128)S(1)}, f32[2,64,128]{2,1,0:T(8,128)S(1)}, u32[]{:S(2)}, u32[]{:S(2)}) collective-permute-start(f32[2,64,128]{2,1,0:T(8,128)S(1)} %get-tuple-element.36), channel_id=1, source_target_pairs={{0,14},{1,5},{2,0},{3,7},{4,2},{5,9},{6,4},{7,11},{8,6},{9,13},{10... | collective-permute-start | bytes 196616 | tf_op jit(solution)/shard_map/ppermute | solution.py:222
  19.4 6.0 %collective-permute-start.7 = (f32[2,64,128]{2,1,0:T(8,128)S(1)}, f32[2,64,128]{2,1,0:T(8,128)S(1)}, u32[]{:S(2)}, u32[]{:S(2)}) collective-permute-start(f32[2,64,128]{2,1,0:T(8,128)S(1)} %get-tuple-element.37), channel_id=1, source_target_pairs={{1,3},{3,5},{5,7},{7,9},{9,11},{11,13},{13,15},{15,1},{17,19},{19,... | collective-permute-start | bytes 196616 | tf_op jit(solution)/shard_map/ppermute | solution.py:222
  25.4 2.9 %collective-permute-start.8 = (f32[2,64,128]{2,1,0:T(8,128)S(1)}, f32[2,64,128]{2,1,0:T(8,128)S(1)}, u32[]{:S(2)}, u32[]{:S(2)}) collective-permute-start(f32[2,64,128]{2,1,0:T(8,128)S(1)} %gather.1.mine_ref), channel_id=1, source_target_pairs={{0,1},{1,0},{2,3},{3,2},{4,5},{5,4},{6,7},{7,6},{8,9},{9,8},{10,11... | collective-permute-start | bytes 196616 | tf_op jit(solution)/shard_map/ppermute | solution.py:226
  29.0 7.7 %collective-permute-start.9 = (f32[80,128]{1,0:T(8,128)S(1)}, f32[80,128]{1,0:T(8,128)S(1)}, u32[]{:S(2)}, u32[]{:S(2)}) collective-permute-start(f32[80,128]{1,0:T(8,128)S(1)} %project.1), channel_id=1, source_target_pairs={{0,32},{32,64},{64,96},{96,128},{128,160},{160,192},{192,224},{224... | collective-permute-start | bytes 122888 | tf_op jit(solution)/shard_map/ppermute | solution.py:235

commit v8 on v7

--- a/solution.py
+++ b/solution.py
@@ -126,20 +126,28 @@
     out_ref[1] = refs[0][1] + refs[1][1] + refs[2][1] + refs[3][1]
 
 
-def project_kernel(mine_ref, beside_ref, projector_ref, other_ref, out_ref):
+def diagonal(packed):
     low = low_lanes((B, 2 * B))
-
-    def diagonal(packed):
-        return jnp.concatenate([jnp.where(low, packed, 0.0), jnp.where(low, 0.0, packed)], axis=0)
-
-    def project(joined, ref):
+    return jnp.concatenate([jnp.where(low, packed, 0.0), jnp.where(low, 0.0, packed)], axis=0)
+
+
+def prepare_kernel(mine_ref, other_ref, right_ref, left_ref):
+    for q, ref in enumerate((mine_ref, other_ref)):
         proj = diagonal(jnp.concatenate([ref[0], ref[1]], axis=1))
-        inner = jnp.dot(diagonal(joined), proj, precision=lax.Precision.HIGHEST, preferred_element_type=F32)
-        full = lax.dot_general(proj, inner, (((0,), (0,)), ((), ())), precision=lax.Precision.HIGHEST, preferred_element_type=F32)
+        right_ref[q] = proj
+        left_ref[q] = proj.T
+
+
+def project_kernel(mine_ref, beside_ref, right_ref, left_ref, out_ref):
+    low = low_lanes((B, 2 * B))
+
+    def project(joined, q):
+        inner = jnp.dot(diagonal(joined), right_ref[q], precision=lax.Precision.HIGHEST, preferred_element_type=F32)
+        full = jnp.dot(left_ref[q], inner, precision=lax.Precision.HIGHEST, preferred_element_type=F32)
         return jnp.where(low, full[:B], full[B:])
 
-    packed = project(mine_ref[0] + beside_ref[1], projector_ref)
-    other = project(mine_ref[1] + beside_ref[0], other_ref)
+    packed = project(mine_ref[0] + beside_ref[1], 0)
+    other = project(mine_ref[1] + beside_ref[0], 1)
     out_ref[pl.ds(0, B), :] = packed
     size = jnp.maximum(jnp.abs(packed), jnp.abs(other))
     top = size[:8]
@@ -210,7 +218,15 @@
     beside = lax.ppermute(message, "core", SWAP)
     projector = projector.reshape(2, B, B)
     other = lax.ppermute(projector, "core", SWAP)
-    over, projector, other = lax.optimization_barrier((over, projector, other))
+    right, left = pl.pallas_call(
+        prepare_kernel,
+        out_shape=[pltpu.VMEM((2, 2 * B, 2 * B), F32)] * 2,
+        in_specs=[VMEM] * 2,
+        out_specs=[VMEM] * 2,
+        compiler_params=SMALL,
+        name="prepare",
+    )(projector, other)
+    over, right, left = lax.optimization_barrier((over, right, left))
     across = lax.ppermute(over, "core", SWAP)
     parts = place((message, beside))
     parts = place((over,), parts)
@@ -231,7 +247,7 @@
         out_specs=VMEM,
         compiler_params=SMALL,
         name="project",
-    )(mine, beside, projector, other)
+    )(mine, beside, right, left)
     moved = lax.ppermute(payload, "col", [(i, (i + 1) % 8) for i in range(8)])
     tops = lax.all_to_all(moved[B:], ("xl", "z"), 0, 0, tiled=True, axis_index_groups=[LEAD])
     return pl.pallas_call(

time: 48.1 us -> 48 us (level)
  no operation moved by 1% of the time
where the time goes in v8:
time: 48 us; the launch traced here: 47.9 us
  starting transfers between devices  15.2 us (32%)
  waiting for transfers between devices  14.6 us (30%)
  blocking collectives  10.5 us (22%)
  Pallas kernels  7.42 us (15%)
    all_to_all x1, blocking collectives, local(): lax.all_to_all(moved[B:], ('xl', 'z'), 0, 0, tiled=True, axis_index_group...  10.5 us
    ppermute x4, starting transfers between devices, along(): return lax.ppermute(x, ('z', 'core'), moves)  8.13 us
    ppermute x1, waiting for transfers between devices, local(): moved = lax.ppermute(payload, 'col', [(i, (i + 1) % 8) for i in range(8)])  5.49 us
    ppermute x4, waiting for transfers between devices, along(): return lax.ppermute(x, ('z', 'core'), moves)  5.38 us
    pallas_call x1, Pallas kernels, local(): pl.pallas_call(products_kernel, out_shape=pltpu.VMEM((MSG + PAIRS, 2 * B)...  4.87 us
    ppermute x1, starting transfers between devices, local(): over = lax.ppermute(message, 'xl', SWAP)  2.36 us
    ppermute x1, starting transfers between devices, local(): moved = lax.ppermute(payload, 'col', [(i, (i + 1) % 8) for i in range(8)])  2.2 us
    ppermute x1, starting transfers between devices, local(): beside = lax.ppermute(mine, 'core', SWAP)  2 us
  transfers between devices with their start and end apart: 10, of which 8 were waited for; matrix products, arithmetic and copies ran while one was open for 0% of the time, Pallas kernels for 2%

profile of v8, /device:TPU:2, one launch (start us, length us, event | category | flops | bytes accessed | tf_op | source)
XLA Modules:
  0.0 47.9 jit_solution(5329518327431411223)
XLA Ops:
  0.0 0.0 copy-start
  0.0 4.9 %products.1.all_refs_0_ = f32[264,128]{1,0:T(8,128)S(1)} custom-call(s32[1,8]{1,0:T(1,128)} %left_hbm.1, s32[1,8]{1,0:T(1,128)} %out_hbm.1, s32[64]{0:T(128)} %owner_hbm.1, bf16[2,4096]{1,0:T(2,128)(2,1)} %bitcast.12, bf16[512,4096]{1,0:T(8,128)(2,1)} %bitcast.9, bf16[512,4096]{1,0:T(8,128)(2,1)} %bitcast.10), custom_call_target="tpu_custom_call" | custom-call | tf_op jit(solution)/shard_map/products/pallas_call | solution.py:195
  4.9 2.4 %collective-permute-start = (f32[264,128]{1,0:T(8,128)S(1)}, f32[264,128]{1,0:T(8,128)S(1)}, u32[]{:S(2)}, u32[]{:S(2)}) collective-permute-start(f32[264,128]{1,0:T(8,128)S(1)} %products.1.all_refs_0_), channel_id=1, source_target_pairs={{0,16},{16,0},{1,17},{17,1},{2,18},{18,2},{3,19},{19,3},{4,20},{20... | collective-permute-start | bytes 405512 | tf_op jit(solution)/shard_map/ppermute | solution.py:217
  7.2 0.0 copy-done
  7.2 0.1 reshape.13.mine_ref
  7.3 0.0 collective-permute-start.1
  7.4 0.5 %collective-permute-start.3 = (f32[264,128]{1,0:T(8,128)S(1)}, f32[264,128]{1,0:T(8,128)S(1)}, u32[]{:S(2)}, u32[]{:S(2)}) collective-permute-start(f32[264,128]{1,0:T(8,128)S(1)} %products.1.all_refs_0_), channel_id=1, source_target_pairs={{0,1},{1,0},{2,3},{3,2},{4,5},{5,4},{6,7},{7,6},{8,9},{9,8},{10,11... | collective-permute-start | bytes 405512 | tf_op jit(solution)/shard_map/ppermute | solution.py:218
  7.9 0.7 %collective-permute-done.1.other_ref = f32[2,64,64]{2,1,0:T(8,128)S(1)} collective-permute-done((f32[2,64,64]{2,1,0:T(8,128)S(1)}, f32[2,64,64]{2,1,0:T(8,128)S(1)}, u32[]{:S(2)}, u32[]{:S(2)}) %collective-permute-start.1) | collective-permute-done | bytes 32800 | tf_op jit(solution)/shard_map/ppermute | solution.py:220
  8.6 0.2 prepare.1
  8.8 1.5 %collective-permute-done.all_refs_0_ = f32[264,128]{1,0:T(8,128)S(1)} collective-permute-done((f32[264,128]{1,0:T(8,128)S(1)}, f32[264,128]{1,0:T(8,128)S(1)}, u32[]{:S(2)}, u32[]{:S(2)}) %collective-permute-start) | collective-permute-done | bytes 135200 | tf_op jit(solution)/shard_map/ppermute | solution.py:217
  10.3 0.0 collective-permute-start.2
  10.3 0.0 collective-permute-done.3.all_refs_1_
  10.3 0.5 place.3
  10.8 0.3 place.4
  11.0 0.6 %collective-permute-done.2.all_refs_0_ = f32[264,128]{1,0:T(8,128)S(1)} collective-permute-done((f32[264,128]{1,0:T(8,128)S(1)}, f32[264,128]{1,0:T(8,128)S(1)}, u32[]{:S(2)}, u32[]{:S(2)}) %collective-permute-start.2) | collective-permute-done | bytes 135200 | tf_op jit(solution)/shard_map/ppermute | solution.py:230
  11.6 0.2 place.5
  11.9 7.3 %collective-permute-start.4 = (f32[2,64,128]{2,1,0:T(8,128)S(1)}, f32[2,64,128]{2,1,0:T(8,128)S(1)}, u32[]{:S(2)}, u32[]{:S(2)}) collective-permute-start(f32[2,64,128]{2,1,0:T(8,128)S(1)} %get-tuple-element.38), channel_id=1, source_target_pairs={{0,8},{1,11},{2,10},{3,13},{4,12},{5,15},{6,14},{7,1},{8,0},{9,3},... | collective-permute-start | bytes 196616 | tf_op jit(solution)/shard_map/ppermute | solution.py:238
  19.2 0.0 collective-permute-start.5
  19.2 0.2 collective-permute-start.6
  19.4 0.7 %collective-permute-start.7 = (f32[2,64,128]{2,1,0:T(8,128)S(1)}, f32[2,64,128]{2,1,0:T(8,128)S(1)}, u32[]{:S(2)}, u32[]{:S(2)}) collective-permute-start(f32[2,64,128]{2,1,0:T(8,128)S(1)} %get-tuple-element.41), channel_id=1, source_target_pairs={{1,3},{3,5},{5,7},{7,9},{9,11},{11,13},{13,15},{15,1},{17,19},{19,... | collective-permute-start | bytes 196616 | tf_op jit(solution)/shard_map/ppermute | solution.py:238
  20.0 1.9 %collective-permute-done.4.refs_0_ = f32[2,64,128]{2,1,0:T(8,128)S(1)} collective-permute-done((f32[2,64,128]{2,1,0:T(8,128)S(1)}, f32[2,64,128]{2,1,0:T(8,128)S(1)}, u32[]{:S(2)}, u32[]{:S(2)}) %collective-permute-start.4) | collective-permute-done | bytes 65568 | tf_op jit(solution)/shard_map/ppermute | solution.py:238
  21.9 3.3 %collective-permute-done.5.refs_1_ = f32[2,64,128]{2,1,0:T(8,128)S(1)} collective-permute-done((f32[2,64,128]{2,1,0:T(8,128)S(1)}, f32[2,64,128]{2,1,0:T(8,128)S(1)}, u32[]{:S(2)}, u32[]{:S(2)}) %collective-permute-start.5) | collective-permute-done | bytes 65568 | tf_op jit(solution)/shard_map/ppermute | solution.py:238
  25.2 0.2 collective-permute-done.6.refs_2_
  25.4 0.0 collective-permute-done.7.refs_3_
  25.4 2.0 %collective-permute-start.8 = (f32[2,64,128]{2,1,0:T(8,128)S(1)}, f32[2,64,128]{2,1,0:T(8,128)S(1)}, u32[]{:S(2)}, u32[]{:S(2)}) collective-permute-start(f32[2,64,128]{2,1,0:T(8,128)S(1)} %gather.1.mine_ref), channel_id=1, source_target_pairs={{0,1},{1,0},{2,3},{3,2},{4,5},{5,4},{6,7},{7,6},{8,9},{9,8},{10,11... | collective-permute-start | bytes 196616 | tf_op jit(solution)/shard_map/ppermute | solution.py:242
  27.4 0.9 %collective-permute-done.8.beside_ref = f32[2,64,128]{2,1,0:T(8,128)S(1)} collective-permute-done((f32[2,64,128]{2,1,0:T(8,128)S(1)}, f32[2,64,128]{2,1,0:T(8,128)S(1)}, u32[]{:S(2)}, u32[]{:S(2)}) %collective-permute-start.8) | collective-permute-done | bytes 65568 | tf_op jit(solution)/shard_map/ppermute | solution.py:242
  28.3 0.6 %project.1 = f32[80,128]{1,0:T(8,128)S(1)} custom-call(f32[2,64,128]{2,1,0:T(8,128)S(1)} %gather.1.mine_ref, f32[2,64,128]{2,1,0:T(8,128)S(1)} %collective-permute-done.8.beside_ref, f32[2,128,128]{2,1,0:T(8,128)S(1)} %get-tuple-element.43.right_ref, f32[2,128,128]{2,1,0:T(8,128)S(1)} %get-tuple-element.44.left_ref), custom_call_target="tpu_custom_call" | custom-call | tf_op jit(solution)/shard_map/project/pallas_call | solution.py:243
  28.9 2.2 %collective-permute-start.9 = (f32[80,128]{1,0:T(8,128)S(1)}, f32[80,128]{1,0:T(8,128)S(1)}, u32[]{:S(2)}, u32[]{:S(2)}) collective-permute-start(f32[80,128]{1,0:T(8,128)S(1)} %project.1), channel_id=1, source_target_pairs={{0,32},{32,64},{64,96},{96,128},{128,160},{160,192},{192,224},{224... | collective-permute-start | bytes 122888 | tf_op jit(solution)/shard_map/ppermute | solution.py:251
  31.1 5.5 %collective-permute-done.9.moved_ref = f32[80,128]{1,0:T(8,128)S(1)} collective-permute-done((f32[80,128]{1,0:T(8,128)S(1)}, f32[80,128]{1,0:T(8,128)S(1)}, u32[]{:S(2)}, u32[]{:S(2)}) %collective-permute-start.9) | collective-permute-done | bytes 40992 | tf_op jit(solution)/shard_map/ppermute | solution.py:251
  36.6 10.5 %all_to_all.11 = f32[16,1,128]{2,1,0:T(1,128)S(1)} all-to-all(f32[16,1,128]{2,1,0:T(1,128)S(1)} %bitcast.11), channel_id=1, replica_groups={{10,26,8,24,6,22,4,20,2,18,0,16,14,30,12,28},{11,27,9,25,7,23,5,21,3,19..., dimensions={0} | all-to-all | bytes 16384 | tf_op jit(solution)/shard_map/all_to_all | solution.py:252
  47.1 0.8 %finish.1 = f32[2,4096]{1,0:T(2,128)} custom-call(f32[80,128]{1,0:T(8,128)S(1)} %collective-permute-done.9.moved_ref, f32[16,128]{1,0:T(8,128)S(1)} %bitcast.8), custom_call_target="tpu_custom_call" | custom-call | tf_op jit(solution)/shard_map/finish/pallas_call | solution.py:253
  (2 shorter events, 0.0 us)
Async XLA Ops:
  0.0 7.2 %copy-start = (f32[1,2,4096]{2,1,0:T(2,128)S(1)}, f32[1,2,4096]{2,1,0:T(2,128)}, u32[]{:S(2)}) copy-start(f32[1,2,4096]{2,1,0:T(2,128)} %param.10) | copy-start | bytes 98308
  4.9 5.4 %collective-permute-start = (f32[264,128]{1,0:T(8,128)S(1)}, f32[264,128]{1,0:T(8,128)S(1)}, u32[]{:S(2)}, u32[]{:S(2)}) collective-permute-start(f32[264,128]{1,0:T(8,128)S(1)} %products.1.all_refs_0_), channel_id=1, source_target_pairs={{0,16},{16,0},{1,17},{17,1},{2,18},{18,2},{3,19},{19,3},{4,20},{20... | collective-permute-start | bytes 405512 | tf_op jit(solution)/shard_map/ppermute | solution.py:217
  7.3 1.3 %collective-permute-start.1 = (f32[2,64,64]{2,1,0:T(8,128)S(1)}, f32[2,64,64]{2,1,0:T(8,128)S(1)}, u32[]{:S(2)}, u32[]{:S(2)}) collective-permute-start(f32[2,64,64]{2,1,0:T(8,128)S(1)} %reshape.13.mine_ref), channel_id=1, source_target_pairs={{0,1},{1,0},{2,3},{3,2},{4,5},{5,4},{6,7},{7,6},{8,9},{9,8},{10,11... | collective-permute-start | bytes 98312 | tf_op jit(solution)/shard_map/ppermute | solution.py:220
  7.4 2.9 %collective-permute-start.3 = (f32[264,128]{1,0:T(8,128)S(1)}, f32[264,128]{1,0:T(8,128)S(1)}, u32[]{:S(2)}, u32[]{:S(2)}) collective-permute-start(f32[264,128]{1,0:T(8,128)S(1)} %products.1.all_refs_0_), channel_id=1, source_target_pairs={{0,1},{1,0},{2,3},{3,2},{4,5},{5,4},{6,7},{7,6},{8,9},{9,8},{10,11... | collective-permute-start | bytes 405512 | tf_op jit(solution)/shard_map/ppermute | solution.py:218
  10.3 1.4 %collective-permute-start.2 = (f32[264,128]{1,0:T(8,128)S(1)}, f32[264,128]{1,0:T(8,128)S(1)}, u32[]{:S(2)}, u32[]{:S(2)}) collective-permute-start(f32[264,128]{1,0:T(8,128)S(1)} %collective-permute-done.all_refs_0_), channel_id=1, source_target_pairs={{0,1},{1,0},{2,3},{3,2},{4,5},{5,4},{6,7},{7,6},{8,9},{9,8},{10,11... | collective-permute-start | bytes 405512 | tf_op jit(solution)/shard_map/ppermute | solution.py:230
  11.9 10.0 %collective-permute-start.4 = (f32[2,64,128]{2,1,0:T(8,128)S(1)}, f32[2,64,128]{2,1,0:T(8,128)S(1)}, u32[]{:S(2)}, u32[]{:S(2)}) collective-permute-start(f32[2,64,128]{2,1,0:T(8,128)S(1)} %get-tuple-element.38), channel_id=1, source_target_pairs={{0,8},{1,11},{2,10},{3,13},{4,12},{5,15},{6,14},{7,1},{8,0},{9,3},... | collective-permute-start | bytes 196616 | tf_op jit(solution)/shard_map/ppermute | solution.py:238
  19.2 6.0 %collective-permute-start.5 = (f32[2,64,128]{2,1,0:T(8,128)S(1)}, f32[2,64,128]{2,1,0:T(8,128)S(1)}, u32[]{:S(2)}, u32[]{:S(2)}) collective-permute-start(f32[2,64,128]{2,1,0:T(8,128)S(1)} %get-tuple-element.39), channel_id=1, source_target_pairs={{0,12},{1,7},{2,14},{3,9},{4,0},{5,11},{6,2},{7,13},{8,4},{9,15},{... | collective-permute-start | bytes 196616 | tf_op jit(solution)/shard_map/ppermute | solution.py:238
  19.2 6.2 %collective-permute-start.6 = (f32[2,64,128]{2,1,0:T(8,128)S(1)}, f32[2,64,128]{2,1,0:T(8,128)S(1)}, u32[]{:S(2)}, u32[]{:S(2)}) collective-permute-start(f32[2,64,128]{2,1,0:T(8,128)S(1)} %get-tuple-element.40), channel_id=1, source_target_pairs={{0,14},{1,5},{2,0},{3,7},{4,2},{5,9},{6,4},{7,11},{8,6},{9,13},{10... | collective-permute-start | bytes 196616 | tf_op jit(solution)/shard_map/ppermute | solution.py:238
  19.4 6.0 %collective-permute-start.7 = (f32[2,64,128]{2,1,0:T(8,128)S(1)}, f32[2,64,128]{2,1,0:T(8,128)S(1)}, u32[]{:S(2)}, u32[]{:S(2)}) collective-permute-start(f32[2,64,128]{2,1,0:T(8,128)S(1)} %get-tuple-element.41), channel_id=1, source_target_pairs={{1,3},{3,5},{5,7},{7,9},{9,11},{11,13},{13,15},{15,1},{17,19},{19,... | collective-permute-start | bytes 196616 | tf_op jit(solution)/shard_map/ppermute | solution.py:238
  25.4 2.9 %collective-permute-start.8 = (f32[2,64,128]{2,1,0:T(8,128)S(1)}, f32[2,64,128]{2,1,0:T(8,128)S(1)}, u32[]{:S(2)}, u32[]{:S(2)}) collective-permute-start(f32[2,64,128]{2,1,0:T(8,128)S(1)} %gather.1.mine_ref), channel_id=1, source_target_pairs={{0,1},{1,0},{2,3},{3,2},{4,5},{5,4},{6,7},{7,6},{8,9},{9,8},{10,11... | collective-permute-start | bytes 196616 | tf_op jit(solution)/shard_map/ppermute | solution.py:242
  28.9 7.7 %collective-permute-start.9 = (f32[80,128]{1,0:T(8,128)S(1)}, f32[80,128]{1,0:T(8,128)S(1)}, u32[]{:S(2)}, u32[]{:S(2)}) collective-permute-start(f32[80,128]{1,0:T(8,128)S(1)} %project.1), channel_id=1, source_target_pairs={{0,32},{32,64},{64,96},{96,128},{128,160},{160,192},{192,224},{224... | collective-permute-start | bytes 122888 | tf_op jit(solution)/shard_map/ppermute | solution.py:251
